TPU v7x, 32 devices: a whole 2x2x4 slice. The times are simulated.
32 devices in a mesh: layer: 2 (over core), rows: 16 (over z, y, x).
Axes of the slice: x: 2, y: 2, z: 4, core: 2. Of those that a mesh axis runs over, the one named last changes fastest.
Arguments:
- frames: bfloat16 [3, 4, 32, 64, 128], P(None, None, 'rows'), may hold values from -6 to 6
- hidden_in: bfloat16 [4, 4, 32, 64, 128], P('layer', None, 'rows'), may hold values from -4 to 4
- cell_in: bfloat16 [4, 4, 32, 64, 128], P('layer', None, 'rows'), may hold values from -6 to 6
- memory_in: bfloat16 [4, 32, 64, 128], P(None, 'rows'), may hold values from -6 to 6
- w_x: bfloat16 [4, 576, 448], P('layer'), may hold values from -0.25 to 0.25
- w_h: bfloat16 [4, 576, 256], P('layer'), may hold values from -0.25 to 0.25
- w_m: bfloat16 [4, 576, 192], P('layer'), may hold values from -0.25 to 0.25
- w_o: bfloat16 [4, 1152, 64], P('layer'), may hold values from -0.1875 to 0.1875
- w_last: bfloat16 [4, 128, 64], P('layer'), may hold values from -0.5 to 0.5
Outputs:
- hidden_out: bfloat16 [4, 4, 32, 64, 128], P('layer', None, 'rows')
- cell_out: bfloat16 [4, 4, 32, 64, 128], P('layer', None, 'rows')
- memory_out: bfloat16 [2, 4, 32, 64, 128], P('layer', None, 'rows')
All inputs are finite; a program needn't handle non-finite values.
Results may differ from a plain program's by a relative error of at most 0.014.
Values may be sent and summed in bfloat16 or wider, within the bound.
A program may use at most 64 MiB of HBM per device.

v0:
```python
import jax
import jax.numpy as jnp
from jax import lax
from jax.sharding import PartitionSpec as P


def shifted(block, axis, distance):
    devices = range(lax.axis_size(axis))
    route = [(i - distance, i) for i in devices if i - distance in devices]
    return lax.ppermute(block, axis, route)


def partner(block, axis, distance):
    count = lax.axis_size(axis)
    route = []
    for low in range(count):
        high = low | 1 << distance
        if high != low and high < count:
            route += [(low, high), (high, low)]
    return lax.ppermute(block, axis, route)


def shifted_taps(padded, height):
    pieces = []
    for row_offset in range(3):
        row_band = padded[:, row_offset : row_offset + height]
        zero_column = jnp.zeros_like(row_band[..., :1])
        pieces.append(jnp.concatenate([zero_column, row_band[..., :-1]], axis=-1))
        pieces.append(row_band)
        pieces.append(jnp.concatenate([row_band[..., 1:], zero_column], axis=-1))
    return jnp.concatenate(pieces, axis=2)


def convolve(padded, weight, height):
    taps = shifted_taps(padded, height)
    return jnp.einsum("ko,brkw->brow", weight, taps, preferred_element_type=jnp.float32)


def gate_math(input_gates, hidden_gates, memory_gates, cell_prev, memory_prev):
    parts_x = jnp.split(input_gates, 7, axis=2)
    parts_h = jnp.split(hidden_gates, 4, axis=2)
    parts_m = jnp.split(memory_gates, 3, axis=2)
    cell_new = (
        jax.nn.sigmoid(parts_x[1] + parts_h[1] + 1.0) * cell_prev.astype(jnp.float32)
        + jax.nn.sigmoid(parts_x[0] + parts_h[0]) * jnp.tanh(parts_x[2] + parts_h[2])
    ).astype(jnp.bfloat16)
    memory_new = (
        jax.nn.sigmoid(parts_x[4] + parts_m[1] + 1.0) * memory_prev.astype(jnp.float32)
        + jax.nn.sigmoid(parts_x[3] + parts_m[0]) * jnp.tanh(parts_x[5] + parts_m[2])
    ).astype(jnp.bfloat16)
    return (cell_new, memory_new, parts_x[6] + parts_h[3])


def band_edges(stacked, width, group):
    above = shifted(stacked[:, :, -width:], "rows", group)
    below = shifted(stacked[:, :, :width], "rows", -group)
    return jnp.concatenate([above, stacked, below], axis=2)


def memory_cell(
    layer_input,
    hidden_prev,
    cell_prev,
    memory_prev,
    weight_x,
    weight_h,
    weight_m,
    weight_o,
    weight_last,
    group,
):
    height = layer_input.shape[1]
    channels = layer_input.shape[2]
    stacked = jnp.stack([layer_input, hidden_prev, memory_prev])
    padded = band_edges(stacked, 1, group)
    input_gates = convolve(padded[0], weight_x, height)
    hidden_gates = convolve(padded[1], weight_h, height)
    memory_gates = convolve(padded[2], weight_m, height)
    cell_new, memory_new, output_part = gate_math(
        input_gates, hidden_gates, memory_gates, cell_prev, memory_prev
    )
    memory_pair = jnp.concatenate([cell_new, memory_new], axis=2)
    padded_pair = band_edges(memory_pair[None], 1, group)[0]
    output_gate = jax.nn.sigmoid(output_part + convolve(padded_pair, weight_o, height))
    mixed = jnp.einsum(
        "ko,brkw->brow", weight_last, memory_pair, preferred_element_type=jnp.float32
    )
    hidden_new = (output_gate * jnp.tanh(mixed)).astype(jnp.bfloat16)
    return (hidden_new, memory_pair[:, :, :channels], memory_pair[:, :, channels:])


def regroup_bundle(bundle, group):
    position = lax.axis_index("rows") % group
    section_count = group.bit_length() - 1
    for section in range(section_count):
        bit_on = position // 2**section % 2 == 1
        depth, count, band, channels, width = bundle.shape
        split_seqs = bundle.reshape(depth, count // 2, 2, band, channels, width)
        keep = jnp.where(bit_on, split_seqs[:, :, 1], split_seqs[:, :, 0])
        send = jnp.where(bit_on, split_seqs[:, :, 0], split_seqs[:, :, 1])
        received = partner(send, "rows", section)
        bundle = jnp.where(
            bit_on,
            jnp.concatenate([received, keep], axis=2),
            jnp.concatenate([keep, received], axis=2),
        )
    return bundle


def ungroup_bundle(bundle, group):
    position = lax.axis_index("rows") % group
    section_count = group.bit_length() - 1
    for section in reversed(range(section_count)):
        bit_on = position // 2**section % 2 == 1
        depth, count, band, channels, width = bundle.shape
        half = band // 2
        keep = jnp.where(bit_on, bundle[:, :, half:], bundle[:, :, :half])
        send = jnp.where(bit_on, bundle[:, :, :half], bundle[:, :, half:])
        received = partner(send, "rows", section)
        paired = jnp.where(
            bit_on, jnp.stack([received, keep], axis=2), jnp.stack([keep, received], axis=2)
        )
        bundle = paired.reshape(depth, count * 2, half, channels, width)
    return bundle


def on_device(frames, hidden_in, cell_in, memory_in, w_x, w_h, w_m, w_o, w_last):
    steps_total = frames.shape[0]
    local_layers = hidden_in.shape[0]
    group = frames.shape[1]
    bundle = jnp.concatenate([frames, hidden_in, cell_in, memory_in[None]], axis=0)
    bundle = regroup_bundle(bundle, group)
    frames = bundle[:steps_total]
    hidden_in = bundle[steps_total : steps_total + local_layers]
    cell_in = bundle[steps_total + local_layers : steps_total + 2 * local_layers]
    memory_in = bundle[steps_total + 2 * local_layers]
    seq_count = frames.shape[1]
    groups = seq_count // seq_count
    job_total = steps_total * groups
    tick_count = 2 * steps_total
    first_section = lax.axis_index("layer") == 0
    anchor_index = jnp.int32(0)
    empty_block = jnp.zeros((seq_count,) + frames.shape[2:], jnp.bfloat16)

    def advance(tick_index, states):
        hidden_loc, cell_loc, wrapped, fwd_hidden, fwd_memory, top_memory = states
        lower_job = tick_index // 2
        lower_active = tick_index % 2 == 0
        upper_job = (tick_index - 1) // 2
        upper_active = tick_index % 2 == 1
        job_index = jnp.clip(
            jnp.where(first_section, lower_job, upper_job), 0, job_total - 1
        ).astype(jnp.int32)
        active = jnp.where(first_section, lower_active, upper_active)
        time_index = job_index // groups
        seq_start = job_index % groups * seq_count
        frame_block = lax.dynamic_index_in_dim(frames, time_index, 0, keepdims=False)
        layer_input = jnp.where(first_section, frame_block, fwd_hidden)
        memory_now = jnp.where(first_section, wrapped, fwd_memory)
        block_shape = (1, seq_count) + hidden_loc.shape[2:]
        for layer_index in range(local_layers):
            corner = (jnp.int32(layer_index), seq_start, anchor_index, anchor_index, anchor_index)
            hidden_prev = lax.dynamic_slice(hidden_loc, corner, block_shape)[0]
            cell_prev = lax.dynamic_slice(cell_loc, corner, block_shape)[0]
            hidden_new, cell_new, memory_new = memory_cell(
                layer_input,
                hidden_prev,
                cell_prev,
                memory_now,
                w_x[layer_index],
                w_h[layer_index],
                w_m[layer_index],
                w_o[layer_index],
                w_last[layer_index],
                group,
            )
            hidden_loc = lax.dynamic_update_slice(
                hidden_loc, jnp.where(active, hidden_new, hidden_prev)[None], corner
            )
            cell_loc = lax.dynamic_update_slice(
                cell_loc, jnp.where(active, cell_new, cell_prev)[None], corner
            )
            layer_input = hidden_new
            memory_now = memory_new
        top_corner = (seq_start, anchor_index, anchor_index, anchor_index)
        top_prev = lax.dynamic_slice(top_memory, top_corner, memory_now.shape)
        top_memory = lax.dynamic_update_slice(
            top_memory, jnp.where(active, memory_now, top_prev), top_corner
        )
        passed_up = shifted(jnp.stack([layer_input, memory_now]), "layer", 1)
        passed_down = shifted(memory_now, "layer", -1)
        upper_index = jnp.clip(upper_job, 0, job_total - 1).astype(jnp.int32)
        upper_start = upper_index % groups * seq_count
        wrap_corner = (upper_start, anchor_index, anchor_index, anchor_index)
        store_wrap = first_section & upper_active
        wrapped_prev = lax.dynamic_slice(wrapped, wrap_corner, passed_down.shape)
        wrapped = lax.dynamic_update_slice(
            wrapped, jnp.where(store_wrap, passed_down, wrapped_prev), wrap_corner
        )
        return (hidden_loc, cell_loc, wrapped, passed_up[0], passed_up[1], top_memory)

    initial = (hidden_in, cell_in, memory_in, empty_block, empty_block, jnp.zeros_like(memory_in))
    finished = lax.fori_loop(0, tick_count, advance, initial)
    hidden_done = finished[0]
    cell_done = finished[1]
    top_done = finished[5][None]
    bundle = jnp.concatenate([hidden_done, cell_done, top_done], axis=0)
    bundle = ungroup_bundle(bundle, group)
    hidden_done = bundle[:local_layers]
    cell_done = bundle[local_layers : 2 * local_layers]
    top_done = bundle[2 * local_layers :]
    return (hidden_done, cell_done, top_done)


def solution(mesh):
    return jax.shard_map(
        on_device,
        mesh=mesh,
        in_specs=(
            P(None, None, "rows", None, None),
            P("layer", None, "rows", None, None),
            P("layer", None, "rows", None, None),
            P(None, "rows", None, None),
            P("layer", None, None),
            P("layer", None, None),
            P("layer", None, None),
            P("layer", None, None),
            P("layer", None, None),
        ),
        out_specs=(
            P("layer", None, "rows", None, None),
            P("layer", None, "rows", None, None),
            P("layer", None, "rows", None, None),
        ),
        check_vma=False,
    )
```

profile of v0, /device:TPU:0, one launch (start us, length us, event | category | flops | bytes accessed | tf_op | source)
XLA Modules:
  0.0 411.1 jit_solution(14352951198393930370)
XLA Ops:
  0.7 1.4 pad_maximum_fusion.13
  2.1 3.0 collective-permute-start.10
  5.2 11.9 %collective-permute-done.10 = bf16[8,2,2,64,128]{4,3,2,1,0:T(8,128)(2,1)S(1)} collective-permute-done((bf16[8,2,2,64,128]{4,3,2,1,0:T(8,128)(2,1)S(1)}, bf16[8,2,2,64,128]{4,3,2,1,0:T(8,128)(2,1)S(1)}, u32[]{:S(2)}, u32[]{:S(2)}) %collective-permute-start.10) | collective-permute-done | bytes 524320 | tf_op jit(solution)/shard_map/ppermute | solution.py:20
  17.2 1.8 collective-permute-start.11
  19.1 11.3 %collective-permute-done.11 = bf16[8,1,4,64,128]{4,3,2,0,1:T(8,128)(2,1)S(1)} collective-permute-done((bf16[8,1,4,64,128]{4,3,2,0,1:T(8,128)(2,1)S(1)}, bf16[8,1,4,64,128]{4,3,2,0,1:T(8,128)(2,1)S(1)}, u32[]{:S(2)}, u32[]{:S(2)}) %collective-permute-start.11) | collective-permute-done | bytes 524320 | tf_op jit(solution)/shard_map/ppermute | solution.py:20
  31.5 356.9 %while.27 = (s32[]{:T(128)}, bf16[2,1,8,64,128]{4,3,2,1,0:T(8,128)(2,1)S(1)}, bf16[2,1,8,64,128]{4,3,2,1,0:T(8,128)(2,1)S(1)}, bf16[1,8,64,128]{3,2,1,0:T(8,128)...) while((s32[]{:T(128)}, ...), condition=%wide.region_1.2_spmd.clone, body=%wide.region_0.1_spmd.clone.sunk | while | flops 2460024832 | bytes 112000408 | solution.py:203
  31.7 1.3 collective-permute-start
  33.0 4.5 %collective-permute-start.1 = (bf16[3,1,1,64,128]{4,3,2,1,0:T(8,128)(2,1)S(1)}, bf16[3,1,1,64,128]{4,3,2,1,0:T(8,128)(2,1)S(1)}, u32[]{:S(2)}, u32[]{:S(2)}) collective-permute-start(bf16[3,1,1,64,128]{4,3,2,1,0:T(8,128)(2,1)S(1)} %get-tuple-element.720), channel_id=1, source_target_pairs={{0,4},{1,5},{2,6},{3,7},{4,8},{5,9},{6,10},{7,11},{8,12},{9,13},{1... | collective-permute-start | bytes 147464 | tf_op jit(solution)/shard_map/while/body/eval_jaxpr/ppermute | solution.py:10
  37.6 1.6 collective-permute-done.1
  44.8 1.3 fusion.205
  48.7 5.5 %collective-permute-start.3 = (bf16[1,1,1,128,128]{4,3,2,1,0:T(8,128)(2,1)}, bf16[1,1,1,128,128]{4,3,2,1,0:T(8,128)(2,1)}, u32[]{:S(2)}, u32[]{:S(2)}) collective-permute-start(bf16[1,1,1,128,128]{4,3,2,1,0:T(8,128)(2,1)} %get-tuple-element.745), channel_id=1, source_target_pairs={{0,4},{1,5},{2,6},{3,7},{4,8},{5,9},{6,10},{7,11},{8,12},{9,13},{1... | collective-permute-start | bytes 98312 | tf_op jit(solution)/shard_map/while/body/eval_jaxpr/ppermute | solution.py:10
  61.0 1.3 collective-permute-start.4
  62.3 4.9 %collective-permute-start.5 = (bf16[3,1,1,64,128]{4,3,2,1,0:T(8,128)(2,1)S(1)}, bf16[3,1,1,64,128]{4,3,2,1,0:T(8,128)(2,1)S(1)}, u32[]{:S(2)}, u32[]{:S(2)}) collective-permute-start(bf16[3,1,1,64,128]{4,3,2,1,0:T(8,128)(2,1)S(1)} %get-tuple-element.755), channel_id=1, source_target_pairs={{0,4},{1,5},{2,6},{3,7},{4,8},{5,9},{6,10},{7,11},{8,12},{9,13},{1... | collective-permute-start | bytes 147464 | tf_op jit(solution)/shard_map/while/body/eval_jaxpr/ppermute | solution.py:10
  67.3 1.6 collective-permute-done.5
  77.6 4.9 %collective-permute-start.7 = (bf16[1,1,1,128,128]{4,3,2,1,0:T(8,128)(2,1)S(1)}, bf16[1,1,1,128,128]{4,3,2,1,0:T(8,128)(2,1)S(1)}, u32[]{:S(2)}, u32[]{:S(2)}) collective-permute-start(bf16[1,1,1,128,128]{4,3,2,1,0:T(8,128)(2,1)S(1)} %get-tuple-element.779), channel_id=1, source_target_pairs={{0,4},{1,5},{2,6},{3,7},{4,8},{5,9},{6,10},{7,11},{8,12},{9,13},{1... | collective-permute-start | bytes 98312 | tf_op jit(solution)/shard_map/while/body/eval_jaxpr/ppermute | solution.py:10
  86.8 2.8 collective-permute-start.9
  92.2 4.6 %collective-permute-start.1 = (bf16[3,1,1,64,128]{4,3,2,1,0:T(8,128)(2,1)S(1)}, bf16[3,1,1,64,128]{4,3,2,1,0:T(8,128)(2,1)S(1)}, u32[]{:S(2)}, u32[]{:S(2)}) collective-permute-start(bf16[3,1,1,64,128]{4,3,2,1,0:T(8,128)(2,1)S(1)} %get-tuple-element.720), channel_id=1, source_target_pairs={{0,4},{1,5},{2,6},{3,7},{4,8},{5,9},{6,10},{7,11},{8,12},{9,13},{1... | collective-permute-start | bytes 147464 | tf_op jit(solution)/shard_map/while/body/eval_jaxpr/ppermute | solution.py:10
  97.1 1.4 collective-permute-done.1
  104.1 1.3 fusion.205
  108.0 5.5 %collective-permute-start.3 = (bf16[1,1,1,128,128]{4,3,2,1,0:T(8,128)(2,1)}, bf16[1,1,1,128,128]{4,3,2,1,0:T(8,128)(2,1)}, u32[]{:S(2)}, u32[]{:S(2)}) collective-permute-start(bf16[1,1,1,128,128]{4,3,2,1,0:T(8,128)(2,1)} %get-tuple-element.745), channel_id=1, source_target_pairs={{0,4},{1,5},{2,6},{3,7},{4,8},{5,9},{6,10},{7,11},{8,12},{9,13},{1... | collective-permute-start | bytes 98312 | tf_op jit(solution)/shard_map/while/body/eval_jaxpr/ppermute | solution.py:10
  121.6 4.9 %collective-permute-start.5 = (bf16[3,1,1,64,128]{4,3,2,1,0:T(8,128)(2,1)S(1)}, bf16[3,1,1,64,128]{4,3,2,1,0:T(8,128)(2,1)S(1)}, u32[]{:S(2)}, u32[]{:S(2)}) collective-permute-start(bf16[3,1,1,64,128]{4,3,2,1,0:T(8,128)(2,1)S(1)} %get-tuple-element.755), channel_id=1, source_target_pairs={{0,4},{1,5},{2,6},{3,7},{4,8},{5,9},{6,10},{7,11},{8,12},{9,13},{1... | collective-permute-start | bytes 147464 | tf_op jit(solution)/shard_map/while/body/eval_jaxpr/ppermute | solution.py:10
  126.6 1.6 collective-permute-done.5
  135.6 1.3 collective-permute-start.6
  136.9 4.9 %collective-permute-start.7 = (bf16[1,1,1,128,128]{4,3,2,1,0:T(8,128)(2,1)S(1)}, bf16[1,1,1,128,128]{4,3,2,1,0:T(8,128)(2,1)S(1)}, u32[]{:S(2)}, u32[]{:S(2)}) collective-permute-start(bf16[1,1,1,128,128]{4,3,2,1,0:T(8,128)(2,1)S(1)} %get-tuple-element.779), channel_id=1, source_target_pairs={{0,4},{1,5},{2,6},{3,7},{4,8},{5,9},{6,10},{7,11},{8,12},{9,13},{1... | collective-permute-start | bytes 98312 | tf_op jit(solution)/shard_map/while/body/eval_jaxpr/ppermute | solution.py:10
  141.8 1.3 collective-permute-start.8
  146.1 2.8 collective-permute-start.9
  151.5 4.8 %collective-permute-start.1 = (bf16[3,1,1,64,128]{4,3,2,1,0:T(8,128)(2,1)S(1)}, bf16[3,1,1,64,128]{4,3,2,1,0:T(8,128)(2,1)S(1)}, u32[]{:S(2)}, u32[]{:S(2)}) collective-permute-start(bf16[3,1,1,64,128]{4,3,2,1,0:T(8,128)(2,1)S(1)} %get-tuple-element.720), channel_id=1, source_target_pairs={{0,4},{1,5},{2,6},{3,7},{4,8},{5,9},{6,10},{7,11},{8,12},{9,13},{1... | collective-permute-start | bytes 147464 | tf_op jit(solution)/shard_map/while/body/eval_jaxpr/ppermute | solution.py:10
  156.7 1.4 collective-permute-done.1
  163.7 1.3 fusion.205
  167.6 5.5 %collective-permute-start.3 = (bf16[1,1,1,128,128]{4,3,2,1,0:T(8,128)(2,1)}, bf16[1,1,1,128,128]{4,3,2,1,0:T(8,128)(2,1)}, u32[]{:S(2)}, u32[]{:S(2)}) collective-permute-start(bf16[1,1,1,128,128]{4,3,2,1,0:T(8,128)(2,1)} %get-tuple-element.745), channel_id=1, source_target_pairs={{0,4},{1,5},{2,6},{3,7},{4,8},{5,9},{6,10},{7,11},{8,12},{9,13},{1... | collective-permute-start | bytes 98312 | tf_op jit(solution)/shard_map/while/body/eval_jaxpr/ppermute | solution.py:10
  181.2 4.9 %collective-permute-start.5 = (bf16[3,1,1,64,128]{4,3,2,1,0:T(8,128)(2,1)S(1)}, bf16[3,1,1,64,128]{4,3,2,1,0:T(8,128)(2,1)S(1)}, u32[]{:S(2)}, u32[]{:S(2)}) collective-permute-start(bf16[3,1,1,64,128]{4,3,2,1,0:T(8,128)(2,1)S(1)} %get-tuple-element.755), channel_id=1, source_target_pairs={{0,4},{1,5},{2,6},{3,7},{4,8},{5,9},{6,10},{7,11},{8,12},{9,13},{1... | collective-permute-start | bytes 147464 | tf_op jit(solution)/shard_map/while/body/eval_jaxpr/ppermute | solution.py:10
  186.2 1.6 collective-permute-done.5
  196.5 4.9 %collective-permute-start.7 = (bf16[1,1,1,128,128]{4,3,2,1,0:T(8,128)(2,1)S(1)}, bf16[1,1,1,128,128]{4,3,2,1,0:T(8,128)(2,1)S(1)}, u32[]{:S(2)}, u32[]{:S(2)}) collective-permute-start(bf16[1,1,1,128,128]{4,3,2,1,0:T(8,128)(2,1)S(1)} %get-tuple-element.779), channel_id=1, source_target_pairs={{0,4},{1,5},{2,6},{3,7},{4,8},{5,9},{6,10},{7,11},{8,12},{9,13},{1... | collective-permute-start | bytes 98312 | tf_op jit(solution)/shard_map/while/body/eval_jaxpr/ppermute | solution.py:10
  205.7 2.8 collective-permute-start.9
  211.1 4.9 %collective-permute-start.1 = (bf16[3,1,1,64,128]{4,3,2,1,0:T(8,128)(2,1)S(1)}, bf16[3,1,1,64,128]{4,3,2,1,0:T(8,128)(2,1)S(1)}, u32[]{:S(2)}, u32[]{:S(2)}) collective-permute-start(bf16[3,1,1,64,128]{4,3,2,1,0:T(8,128)(2,1)S(1)} %get-tuple-element.720), channel_id=1, source_target_pairs={{0,4},{1,5},{2,6},{3,7},{4,8},{5,9},{6,10},{7,11},{8,12},{9,13},{1... | collective-permute-start | bytes 147464 | tf_op jit(solution)/shard_map/while/body/eval_jaxpr/ppermute | solution.py:10
  216.3 1.4 collective-permute-done.1
  223.3 1.3 fusion.205
  227.2 5.5 %collective-permute-start.3 = (bf16[1,1,1,128,128]{4,3,2,1,0:T(8,128)(2,1)}, bf16[1,1,1,128,128]{4,3,2,1,0:T(8,128)(2,1)}, u32[]{:S(2)}, u32[]{:S(2)}) collective-permute-start(bf16[1,1,1,128,128]{4,3,2,1,0:T(8,128)(2,1)} %get-tuple-element.745), channel_id=1, source_target_pairs={{0,4},{1,5},{2,6},{3,7},{4,8},{5,9},{6,10},{7,11},{8,12},{9,13},{1... | collective-permute-start | bytes 98312 | tf_op jit(solution)/shard_map/while/body/eval_jaxpr/ppermute | solution.py:10
  240.8 4.9 %collective-permute-start.5 = (bf16[3,1,1,64,128]{4,3,2,1,0:T(8,128)(2,1)S(1)}, bf16[3,1,1,64,128]{4,3,2,1,0:T(8,128)(2,1)S(1)}, u32[]{:S(2)}, u32[]{:S(2)}) collective-permute-start(bf16[3,1,1,64,128]{4,3,2,1,0:T(8,128)(2,1)S(1)} %get-tuple-element.755), channel_id=1, source_target_pairs={{0,4},{1,5},{2,6},{3,7},{4,8},{5,9},{6,10},{7,11},{8,12},{9,13},{1... | collective-permute-start | bytes 147464 | tf_op jit(solution)/shard_map/while/body/eval_jaxpr/ppermute | solution.py:10
  245.8 1.6 collective-permute-done.5
  256.1 4.9 %collective-permute-start.7 = (bf16[1,1,1,128,128]{4,3,2,1,0:T(8,128)(2,1)S(1)}, bf16[1,1,1,128,128]{4,3,2,1,0:T(8,128)(2,1)S(1)}, u32[]{:S(2)}, u32[]{:S(2)}) collective-permute-start(bf16[1,1,1,128,128]{4,3,2,1,0:T(8,128)(2,1)S(1)} %get-tuple-element.779), channel_id=1, source_target_pairs={{0,4},{1,5},{2,6},{3,7},{4,8},{5,9},{6,10},{7,11},{8,12},{9,13},{1... | collective-permute-start | bytes 98312 | tf_op jit(solution)/shard_map/while/body/eval_jaxpr/ppermute | solution.py:10
  265.2 2.8 collective-permute-start.9
  270.7 4.9 %collective-permute-start.1 = (bf16[3,1,1,64,128]{4,3,2,1,0:T(8,128)(2,1)S(1)}, bf16[3,1,1,64,128]{4,3,2,1,0:T(8,128)(2,1)S(1)}, u32[]{:S(2)}, u32[]{:S(2)}) collective-permute-start(bf16[3,1,1,64,128]{4,3,2,1,0:T(8,128)(2,1)S(1)} %get-tuple-element.720), channel_id=1, source_target_pairs={{0,4},{1,5},{2,6},{3,7},{4,8},{5,9},{6,10},{7,11},{8,12},{9,13},{1... | collective-permute-start | bytes 147464 | tf_op jit(solution)/shard_map/while/body/eval_jaxpr/ppermute | solution.py:10
  275.9 1.4 collective-permute-done.1
  282.8 1.3 fusion.205
  286.8 5.5 %collective-permute-start.3 = (bf16[1,1,1,128,128]{4,3,2,1,0:T(8,128)(2,1)}, bf16[1,1,1,128,128]{4,3,2,1,0:T(8,128)(2,1)}, u32[]{:S(2)}, u32[]{:S(2)}) collective-permute-start(bf16[1,1,1,128,128]{4,3,2,1,0:T(8,128)(2,1)} %get-tuple-element.745), channel_id=1, source_target_pairs={{0,4},{1,5},{2,6},{3,7},{4,8},{5,9},{6,10},{7,11},{8,12},{9,13},{1... | collective-permute-start | bytes 98312 | tf_op jit(solution)/shard_map/while/body/eval_jaxpr/ppermute | solution.py:10
  299.1 1.3 collective-permute-start.4
  300.4 4.9 %collective-permute-start.5 = (bf16[3,1,1,64,128]{4,3,2,1,0:T(8,128)(2,1)S(1)}, bf16[3,1,1,64,128]{4,3,2,1,0:T(8,128)(2,1)S(1)}, u32[]{:S(2)}, u32[]{:S(2)}) collective-permute-start(bf16[3,1,1,64,128]{4,3,2,1,0:T(8,128)(2,1)S(1)} %get-tuple-element.755), channel_id=1, source_target_pairs={{0,4},{1,5},{2,6},{3,7},{4,8},{5,9},{6,10},{7,11},{8,12},{9,13},{1... | collective-permute-start | bytes 147464 | tf_op jit(solution)/shard_map/while/body/eval_jaxpr/ppermute | solution.py:10
  305.3 1.6 collective-permute-done.5
  315.7 4.9 %collective-permute-start.7 = (bf16[1,1,1,128,128]{4,3,2,1,0:T(8,128)(2,1)S(1)}, bf16[1,1,1,128,128]{4,3,2,1,0:T(8,128)(2,1)S(1)}, u32[]{:S(2)}, u32[]{:S(2)}) collective-permute-start(bf16[1,1,1,128,128]{4,3,2,1,0:T(8,128)(2,1)S(1)} %get-tuple-element.779), channel_id=1, source_target_pairs={{0,4},{1,5},{2,6},{3,7},{4,8},{5,9},{6,10},{7,11},{8,12},{9,13},{1... | collective-permute-start | bytes 98312 | tf_op jit(solution)/shard_map/while/body/eval_jaxpr/ppermute | solution.py:10
  324.8 2.8 collective-permute-start.9
  330.3 4.9 %collective-permute-start.1 = (bf16[3,1,1,64,128]{4,3,2,1,0:T(8,128)(2,1)S(1)}, bf16[3,1,1,64,128]{4,3,2,1,0:T(8,128)(2,1)S(1)}, u32[]{:S(2)}, u32[]{:S(2)}) collective-permute-start(bf16[3,1,1,64,128]{4,3,2,1,0:T(8,128)(2,1)S(1)} %get-tuple-element.720), channel_id=1, source_target_pairs={{0,4},{1,5},{2,6},{3,7},{4,8},{5,9},{6,10},{7,11},{8,12},{9,13},{1... | collective-permute-start | bytes 147464 | tf_op jit(solution)/shard_map/while/body/eval_jaxpr/ppermute | solution.py:10
  335.5 1.4 collective-permute-done.1
  342.4 1.3 fusion.205
  346.4 5.5 %collective-permute-start.3 = (bf16[1,1,1,128,128]{4,3,2,1,0:T(8,128)(2,1)}, bf16[1,1,1,128,128]{4,3,2,1,0:T(8,128)(2,1)}, u32[]{:S(2)}, u32[]{:S(2)}) collective-permute-start(bf16[1,1,1,128,128]{4,3,2,1,0:T(8,128)(2,1)} %get-tuple-element.745), channel_id=1, source_target_pairs={{0,4},{1,5},{2,6},{3,7},{4,8},{5,9},{6,10},{7,11},{8,12},{9,13},{1... | collective-permute-start | bytes 98312 | tf_op jit(solution)/shard_map/while/body/eval_jaxpr/ppermute | solution.py:10
  358.6 1.3 collective-permute-start.4
  359.9 4.9 %collective-permute-start.5 = (bf16[3,1,1,64,128]{4,3,2,1,0:T(8,128)(2,1)S(1)}, bf16[3,1,1,64,128]{4,3,2,1,0:T(8,128)(2,1)S(1)}, u32[]{:S(2)}, u32[]{:S(2)}) collective-permute-start(bf16[3,1,1,64,128]{4,3,2,1,0:T(8,128)(2,1)S(1)} %get-tuple-element.755), channel_id=1, source_target_pairs={{0,4},{1,5},{2,6},{3,7},{4,8},{5,9},{6,10},{7,11},{8,12},{9,13},{1... | collective-permute-start | bytes 147464 | tf_op jit(solution)/shard_map/while/body/eval_jaxpr/ppermute | solution.py:10
  364.9 1.6 collective-permute-done.5
  375.3 4.9 %collective-permute-start.7 = (bf16[1,1,1,128,128]{4,3,2,1,0:T(8,128)(2,1)S(1)}, bf16[1,1,1,128,128]{4,3,2,1,0:T(8,128)(2,1)S(1)}, u32[]{:S(2)}, u32[]{:S(2)}) collective-permute-start(bf16[1,1,1,128,128]{4,3,2,1,0:T(8,128)(2,1)S(1)} %get-tuple-element.779), channel_id=1, source_target_pairs={{0,4},{1,5},{2,6},{3,7},{4,8},{5,9},{6,10},{7,11},{8,12},{9,13},{1... | collective-permute-start | bytes 98312 | tf_op jit(solution)/shard_map/while/body/eval_jaxpr/ppermute | solution.py:10
  384.4 2.8 collective-permute-start.9
  389.4 1.5 collective-permute-start.12
  391.0 8.5 %collective-permute-done.12 = bf16[5,1,4,64,128]{4,3,2,1,0:T(8,128)(2,1)S(1)} collective-permute-done((bf16[5,1,4,64,128]{4,3,2,1,0:T(8,128)(2,1)S(1)}, bf16[5,1,4,64,128]{4,3,2,1,0:T(8,128)(2,1)S(1)}, u32[]{:S(2)}, u32[]{:S(2)}) %collective-permute-start.12) | collective-permute-done | bytes 327712 | tf_op jit(solution)/shard_map/ppermute | solution.py:20
  399.6 1.5 collective-permute-start.13
  401.1 7.8 %collective-permute-done.13 = bf16[5,2,2,64,128]{4,3,2,1,0:T(8,128)(2,1)S(1)} collective-permute-done((bf16[5,2,2,64,128]{4,3,2,1,0:T(8,128)(2,1)S(1)}, bf16[5,2,2,64,128]{4,3,2,1,0:T(8,128)(2,1)S(1)}, u32[]{:S(2)}, u32[]{:S(2)}) %collective-permute-start.13) | collective-permute-done | bytes 327712 | tf_op jit(solution)/shard_map/ppermute | solution.py:20
  (996 shorter events, 185.2 us)
Async XLA Ops:
  2.1 14.9 %collective-permute-start.10 = (bf16[8,2,2,64,128]{4,3,2,1,0:T(8,128)(2,1)S(1)}, bf16[8,2,2,64,128]{4,3,2,1,0:T(8,128)(2,1)S(1)}, u32[]{:S(2)}, u32[]{:S(2)}) collective-permute-start(bf16[8,2,2,64,128]{4,3,2,1,0:T(8,128)(2,1)S(1)} %fusion.139), channel_id=1, source_target_pairs={{0,1},{1,0},{2,3},{3,2},{4,5},{5,4},{6,7},{7,6},{8,9},{9,8},{10,11... | collective-permute-start | bytes 1572872 | tf_op jit(solution)/shard_map/ppermute | solution.py:20
  17.2 13.2 %collective-permute-start.11 = (bf16[8,1,4,64,128]{4,3,2,0,1:T(8,128)(2,1)S(1)}, bf16[8,1,4,64,128]{4,3,2,0,1:T(8,128)(2,1)S(1)}, u32[]{:S(2)}, u32[]{:S(2)}) collective-permute-start(bf16[8,1,4,64,128]{4,3,2,0,1:T(8,128)(2,1)S(1)} %fusion.138), channel_id=1, source_target_pairs={{0,2},{2,0},{1,3},{3,1},{4,6},{6,4},{5,7},{7,5},{8,10},{10,8},{9,1... | collective-permute-start | bytes 1572872 | tf_op jit(solution)/shard_map/ppermute | solution.py:20
  31.7 6.0 %collective-permute-start = (bf16[3,1,1,64,128]{4,3,2,1,0:T(8,128)(2,1)S(1)}, bf16[3,1,1,64,128]{4,3,2,1,0:T(8,128)(2,1)S(1)}, u32[]{:S(2)}, u32[]{:S(2)}) collective-permute-start(bf16[3,1,1,64,128]{4,3,2,1,0:T(8,128)(2,1)S(1)} %get-tuple-element.719), channel_id=1, source_target_pairs={{4,0},{5,1},{6,2},{7,3},{8,4},{9,5},{10,6},{11,7},{12,8},{13,9},{1... | collective-permute-start | bytes 147464 | tf_op jit(solution)/shard_map/while/body/eval_jaxpr/ppermute | solution.py:10
  33.0 6.3 %collective-permute-start.1 = (bf16[3,1,1,64,128]{4,3,2,1,0:T(8,128)(2,1)S(1)}, bf16[3,1,1,64,128]{4,3,2,1,0:T(8,128)(2,1)S(1)}, u32[]{:S(2)}, u32[]{:S(2)}) collective-permute-start(bf16[3,1,1,64,128]{4,3,2,1,0:T(8,128)(2,1)S(1)} %get-tuple-element.720), channel_id=1, source_target_pairs={{0,4},{1,5},{2,6},{3,7},{4,8},{5,9},{6,10},{7,11},{8,12},{9,13},{1... | collective-permute-start | bytes 147464 | tf_op jit(solution)/shard_map/while/body/eval_jaxpr/ppermute | solution.py:10
  47.5 7.4 %collective-permute-start.2 = (bf16[1,1,1,128,128]{4,3,2,1,0:T(8,128)(2,1)}, bf16[1,1,1,128,128]{4,3,2,1,0:T(8,128)(2,1)}, u32[]{:S(2)}, u32[]{:S(2)}) collective-permute-start(bf16[1,1,1,128,128]{4,3,2,1,0:T(8,128)(2,1)} %get-tuple-element.744), channel_id=1, source_target_pairs={{4,0},{5,1},{6,2},{7,3},{8,4},{9,5},{10,6},{11,7},{12,8},{13,9},{1... | collective-permute-start | bytes 98312 | tf_op jit(solution)/shard_map/while/body/eval_jaxpr/ppermute | solution.py:10
  48.7 6.8 %collective-permute-start.3 = (bf16[1,1,1,128,128]{4,3,2,1,0:T(8,128)(2,1)}, bf16[1,1,1,128,128]{4,3,2,1,0:T(8,128)(2,1)}, u32[]{:S(2)}, u32[]{:S(2)}) collective-permute-start(bf16[1,1,1,128,128]{4,3,2,1,0:T(8,128)(2,1)} %get-tuple-element.745), channel_id=1, source_target_pairs={{0,4},{1,5},{2,6},{3,7},{4,8},{5,9},{6,10},{7,11},{8,12},{9,13},{1... | collective-permute-start | bytes 98312 | tf_op jit(solution)/shard_map/while/body/eval_jaxpr/ppermute | solution.py:10
  61.0 6.3 %collective-permute-start.4 = (bf16[3,1,1,64,128]{4,3,2,1,0:T(8,128)(2,1)S(1)}, bf16[3,1,1,64,128]{4,3,2,1,0:T(8,128)(2,1)S(1)}, u32[]{:S(2)}, u32[]{:S(2)}) collective-permute-start(bf16[3,1,1,64,128]{4,3,2,1,0:T(8,128)(2,1)S(1)} %get-tuple-element.754), channel_id=1, source_target_pairs={{4,0},{5,1},{6,2},{7,3},{8,4},{9,5},{10,6},{11,7},{12,8},{13,9},{1... | collective-permute-start | bytes 147464 | tf_op jit(solution)/shard_map/while/body/eval_jaxpr/ppermute | solution.py:10
  62.3 6.6 %collective-permute-start.5 = (bf16[3,1,1,64,128]{4,3,2,1,0:T(8,128)(2,1)S(1)}, bf16[3,1,1,64,128]{4,3,2,1,0:T(8,128)(2,1)S(1)}, u32[]{:S(2)}, u32[]{:S(2)}) collective-permute-start(bf16[3,1,1,64,128]{4,3,2,1,0:T(8,128)(2,1)S(1)} %get-tuple-element.755), channel_id=1, source_target_pairs={{0,4},{1,5},{2,6},{3,7},{4,8},{5,9},{6,10},{7,11},{8,12},{9,13},{1... | collective-permute-start | bytes 147464 | tf_op jit(solution)/shard_map/while/body/eval_jaxpr/ppermute | solution.py:10
  76.3 7.5 %collective-permute-start.6 = (bf16[1,1,1,128,128]{4,3,2,1,0:T(8,128)(2,1)S(1)}, bf16[1,1,1,128,128]{4,3,2,1,0:T(8,128)(2,1)S(1)}, u32[]{:S(2)}, u32[]{:S(2)}) collective-permute-start(bf16[1,1,1,128,128]{4,3,2,1,0:T(8,128)(2,1)S(1)} %get-tuple-element.778), channel_id=1, source_target_pairs={{4,0},{5,1},{6,2},{7,3},{8,4},{9,5},{10,6},{11,7},{12,8},{13,9},{1... | collective-permute-start | bytes 98312 | tf_op jit(solution)/shard_map/while/body/eval_jaxpr/ppermute | solution.py:10
  77.6 6.5 %collective-permute-start.7 = (bf16[1,1,1,128,128]{4,3,2,1,0:T(8,128)(2,1)S(1)}, bf16[1,1,1,128,128]{4,3,2,1,0:T(8,128)(2,1)S(1)}, u32[]{:S(2)}, u32[]{:S(2)}) collective-permute-start(bf16[1,1,1,128,128]{4,3,2,1,0:T(8,128)(2,1)S(1)} %get-tuple-element.779), channel_id=1, source_target_pairs={{0,4},{1,5},{2,6},{3,7},{4,8},{5,9},{6,10},{7,11},{8,12},{9,13},{1... | collective-permute-start | bytes 98312 | tf_op jit(solution)/shard_map/while/body/eval_jaxpr/ppermute | solution.py:10
  82.5 7.1 %collective-permute-start.8 = (bf16[1,8,64,128]{3,2,1,0:T(8,128)(2,1)S(1)}, bf16[1,8,64,128]{3,2,1,0:T(8,128)(2,1)S(1)}, u32[]{:S(2)}, u32[]{:S(2)}) collective-permute-start(bf16[1,8,64,128]{3,2,1,0:T(8,128)(2,1)S(1)} %get-tuple-element.770), channel_id=1, source_target_pairs={{16,0},{17,1},{18,2},{19,3},{20,4},{21,5},{22,6},{23,7},{24,8},{25... | collective-permute-start | bytes 393224 | tf_op jit(solution)/shard_map/while/body/eval_jaxpr/ppermute | solution.py:10
  86.8 4.0 collective-permute-start.9
  90.9 6.2 %collective-permute-start = (bf16[3,1,1,64,128]{4,3,2,1,0:T(8,128)(2,1)S(1)}, bf16[3,1,1,64,128]{4,3,2,1,0:T(8,128)(2,1)S(1)}, u32[]{:S(2)}, u32[]{:S(2)}) collective-permute-start(bf16[3,1,1,64,128]{4,3,2,1,0:T(8,128)(2,1)S(1)} %get-tuple-element.719), channel_id=1, source_target_pairs={{4,0},{5,1},{6,2},{7,3},{8,4},{9,5},{10,6},{11,7},{12,8},{13,9},{1... | collective-permute-start | bytes 147464 | tf_op jit(solution)/shard_map/while/body/eval_jaxpr/ppermute | solution.py:10
  92.2 6.3 %collective-permute-start.1 = (bf16[3,1,1,64,128]{4,3,2,1,0:T(8,128)(2,1)S(1)}, bf16[3,1,1,64,128]{4,3,2,1,0:T(8,128)(2,1)S(1)}, u32[]{:S(2)}, u32[]{:S(2)}) collective-permute-start(bf16[3,1,1,64,128]{4,3,2,1,0:T(8,128)(2,1)S(1)} %get-tuple-element.720), channel_id=1, source_target_pairs={{0,4},{1,5},{2,6},{3,7},{4,8},{5,9},{6,10},{7,11},{8,12},{9,13},{1... | collective-permute-start | bytes 147464 | tf_op jit(solution)/shard_map/while/body/eval_jaxpr/ppermute | solution.py:10
  106.8 7.4 %collective-permute-start.2 = (bf16[1,1,1,128,128]{4,3,2,1,0:T(8,128)(2,1)}, bf16[1,1,1,128,128]{4,3,2,1,0:T(8,128)(2,1)}, u32[]{:S(2)}, u32[]{:S(2)}) collective-permute-start(bf16[1,1,1,128,128]{4,3,2,1,0:T(8,128)(2,1)} %get-tuple-element.744), channel_id=1, source_target_pairs={{4,0},{5,1},{6,2},{7,3},{8,4},{9,5},{10,6},{11,7},{12,8},{13,9},{1... | collective-permute-start | bytes 98312 | tf_op jit(solution)/shard_map/while/body/eval_jaxpr/ppermute | solution.py:10
  108.0 6.8 %collective-permute-start.3 = (bf16[1,1,1,128,128]{4,3,2,1,0:T(8,128)(2,1)}, bf16[1,1,1,128,128]{4,3,2,1,0:T(8,128)(2,1)}, u32[]{:S(2)}, u32[]{:S(2)}) collective-permute-start(bf16[1,1,1,128,128]{4,3,2,1,0:T(8,128)(2,1)} %get-tuple-element.745), channel_id=1, source_target_pairs={{0,4},{1,5},{2,6},{3,7},{4,8},{5,9},{6,10},{7,11},{8,12},{9,13},{1... | collective-permute-start | bytes 98312 | tf_op jit(solution)/shard_map/while/body/eval_jaxpr/ppermute | solution.py:10
  120.3 6.3 %collective-permute-start.4 = (bf16[3,1,1,64,128]{4,3,2,1,0:T(8,128)(2,1)S(1)}, bf16[3,1,1,64,128]{4,3,2,1,0:T(8,128)(2,1)S(1)}, u32[]{:S(2)}, u32[]{:S(2)}) collective-permute-start(bf16[3,1,1,64,128]{4,3,2,1,0:T(8,128)(2,1)S(1)} %get-tuple-element.754), channel_id=1, source_target_pairs={{4,0},{5,1},{6,2},{7,3},{8,4},{9,5},{10,6},{11,7},{12,8},{13,9},{1... | collective-permute-start | bytes 147464 | tf_op jit(solution)/shard_map/while/body/eval_jaxpr/ppermute | solution.py:10
  121.6 6.6 %collective-permute-start.5 = (bf16[3,1,1,64,128]{4,3,2,1,0:T(8,128)(2,1)S(1)}, bf16[3,1,1,64,128]{4,3,2,1,0:T(8,128)(2,1)S(1)}, u32[]{:S(2)}, u32[]{:S(2)}) collective-permute-start(bf16[3,1,1,64,128]{4,3,2,1,0:T(8,128)(2,1)S(1)} %get-tuple-element.755), channel_id=1, source_target_pairs={{0,4},{1,5},{2,6},{3,7},{4,8},{5,9},{6,10},{7,11},{8,12},{9,13},{1... | collective-permute-start | bytes 147464 | tf_op jit(solution)/shard_map/while/body/eval_jaxpr/ppermute | solution.py:10
  135.6 7.5 %collective-permute-start.6 = (bf16[1,1,1,128,128]{4,3,2,1,0:T(8,128)(2,1)S(1)}, bf16[1,1,1,128,128]{4,3,2,1,0:T(8,128)(2,1)S(1)}, u32[]{:S(2)}, u32[]{:S(2)}) collective-permute-start(bf16[1,1,1,128,128]{4,3,2,1,0:T(8,128)(2,1)S(1)} %get-tuple-element.778), channel_id=1, source_target_pairs={{4,0},{5,1},{6,2},{7,3},{8,4},{9,5},{10,6},{11,7},{12,8},{13,9},{1... | collective-permute-start | bytes 98312 | tf_op jit(solution)/shard_map/while/body/eval_jaxpr/ppermute | solution.py:10
  136.9 6.5 %collective-permute-start.7 = (bf16[1,1,1,128,128]{4,3,2,1,0:T(8,128)(2,1)S(1)}, bf16[1,1,1,128,128]{4,3,2,1,0:T(8,128)(2,1)S(1)}, u32[]{:S(2)}, u32[]{:S(2)}) collective-permute-start(bf16[1,1,1,128,128]{4,3,2,1,0:T(8,128)(2,1)S(1)} %get-tuple-element.779), channel_id=1, source_target_pairs={{0,4},{1,5},{2,6},{3,7},{4,8},{5,9},{6,10},{7,11},{8,12},{9,13},{1... | collective-permute-start | bytes 98312 | tf_op jit(solution)/shard_map/while/body/eval_jaxpr/ppermute | solution.py:10
  141.8 7.1 %collective-permute-start.8 = (bf16[1,8,64,128]{3,2,1,0:T(8,128)(2,1)S(1)}, bf16[1,8,64,128]{3,2,1,0:T(8,128)(2,1)S(1)}, u32[]{:S(2)}, u32[]{:S(2)}) collective-permute-start(bf16[1,8,64,128]{3,2,1,0:T(8,128)(2,1)S(1)} %get-tuple-element.770), channel_id=1, source_target_pairs={{16,0},{17,1},{18,2},{19,3},{20,4},{21,5},{22,6},{23,7},{24,8},{25... | collective-permute-start | bytes 393224 | tf_op jit(solution)/shard_map/while/body/eval_jaxpr/ppermute | solution.py:10
  146.1 4.0 collective-permute-start.9
  150.2 6.5 %collective-permute-start = (bf16[3,1,1,64,128]{4,3,2,1,0:T(8,128)(2,1)S(1)}, bf16[3,1,1,64,128]{4,3,2,1,0:T(8,128)(2,1)S(1)}, u32[]{:S(2)}, u32[]{:S(2)}) collective-permute-start(bf16[3,1,1,64,128]{4,3,2,1,0:T(8,128)(2,1)S(1)} %get-tuple-element.719), channel_id=1, source_target_pairs={{4,0},{5,1},{6,2},{7,3},{8,4},{9,5},{10,6},{11,7},{12,8},{13,9},{1... | collective-permute-start | bytes 147464 | tf_op jit(solution)/shard_map/while/body/eval_jaxpr/ppermute | solution.py:10
  151.5 6.6 %collective-permute-start.1 = (bf16[3,1,1,64,128]{4,3,2,1,0:T(8,128)(2,1)S(1)}, bf16[3,1,1,64,128]{4,3,2,1,0:T(8,128)(2,1)S(1)}, u32[]{:S(2)}, u32[]{:S(2)}) collective-permute-start(bf16[3,1,1,64,128]{4,3,2,1,0:T(8,128)(2,1)S(1)} %get-tuple-element.720), channel_id=1, source_target_pairs={{0,4},{1,5},{2,6},{3,7},{4,8},{5,9},{6,10},{7,11},{8,12},{9,13},{1... | collective-permute-start | bytes 147464 | tf_op jit(solution)/shard_map/while/body/eval_jaxpr/ppermute | solution.py:10
  166.3 7.4 %collective-permute-start.2 = (bf16[1,1,1,128,128]{4,3,2,1,0:T(8,128)(2,1)}, bf16[1,1,1,128,128]{4,3,2,1,0:T(8,128)(2,1)}, u32[]{:S(2)}, u32[]{:S(2)}) collective-permute-start(bf16[1,1,1,128,128]{4,3,2,1,0:T(8,128)(2,1)} %get-tuple-element.744), channel_id=1, source_target_pairs={{4,0},{5,1},{6,2},{7,3},{8,4},{9,5},{10,6},{11,7},{12,8},{13,9},{1... | collective-permute-start | bytes 98312 | tf_op jit(solution)/shard_map/while/body/eval_jaxpr/ppermute | solution.py:10
  167.6 6.8 %collective-permute-start.3 = (bf16[1,1,1,128,128]{4,3,2,1,0:T(8,128)(2,1)}, bf16[1,1,1,128,128]{4,3,2,1,0:T(8,128)(2,1)}, u32[]{:S(2)}, u32[]{:S(2)}) collective-permute-start(bf16[1,1,1,128,128]{4,3,2,1,0:T(8,128)(2,1)} %get-tuple-element.745), channel_id=1, source_target_pairs={{0,4},{1,5},{2,6},{3,7},{4,8},{5,9},{6,10},{7,11},{8,12},{9,13},{1... | collective-permute-start | bytes 98312 | tf_op jit(solution)/shard_map/while/body/eval_jaxpr/ppermute | solution.py:10
  179.9 6.3 %collective-permute-start.4 = (bf16[3,1,1,64,128]{4,3,2,1,0:T(8,128)(2,1)S(1)}, bf16[3,1,1,64,128]{4,3,2,1,0:T(8,128)(2,1)S(1)}, u32[]{:S(2)}, u32[]{:S(2)}) collective-permute-start(bf16[3,1,1,64,128]{4,3,2,1,0:T(8,128)(2,1)S(1)} %get-tuple-element.754), channel_id=1, source_target_pairs={{4,0},{5,1},{6,2},{7,3},{8,4},{9,5},{10,6},{11,7},{12,8},{13,9},{1... | collective-permute-start | bytes 147464 | tf_op jit(solution)/shard_map/while/body/eval_jaxpr/ppermute | solution.py:10
  181.2 6.6 %collective-permute-start.5 = (bf16[3,1,1,64,128]{4,3,2,1,0:T(8,128)(2,1)S(1)}, bf16[3,1,1,64,128]{4,3,2,1,0:T(8,128)(2,1)S(1)}, u32[]{:S(2)}, u32[]{:S(2)}) collective-permute-start(bf16[3,1,1,64,128]{4,3,2,1,0:T(8,128)(2,1)S(1)} %get-tuple-element.755), channel_id=1, source_target_pairs={{0,4},{1,5},{2,6},{3,7},{4,8},{5,9},{6,10},{7,11},{8,12},{9,13},{1... | collective-permute-start | bytes 147464 | tf_op jit(solution)/shard_map/while/body/eval_jaxpr/ppermute | solution.py:10
  195.2 7.5 %collective-permute-start.6 = (bf16[1,1,1,128,128]{4,3,2,1,0:T(8,128)(2,1)S(1)}, bf16[1,1,1,128,128]{4,3,2,1,0:T(8,128)(2,1)S(1)}, u32[]{:S(2)}, u32[]{:S(2)}) collective-permute-start(bf16[1,1,1,128,128]{4,3,2,1,0:T(8,128)(2,1)S(1)} %get-tuple-element.778), channel_id=1, source_target_pairs={{4,0},{5,1},{6,2},{7,3},{8,4},{9,5},{10,6},{11,7},{12,8},{13,9},{1... | collective-permute-start | bytes 98312 | tf_op jit(solution)/shard_map/while/body/eval_jaxpr/ppermute | solution.py:10
  196.5 6.5 %collective-permute-start.7 = (bf16[1,1,1,128,128]{4,3,2,1,0:T(8,128)(2,1)S(1)}, bf16[1,1,1,128,128]{4,3,2,1,0:T(8,128)(2,1)S(1)}, u32[]{:S(2)}, u32[]{:S(2)}) collective-permute-start(bf16[1,1,1,128,128]{4,3,2,1,0:T(8,128)(2,1)S(1)} %get-tuple-element.779), channel_id=1, source_target_pairs={{0,4},{1,5},{2,6},{3,7},{4,8},{5,9},{6,10},{7,11},{8,12},{9,13},{1... | collective-permute-start | bytes 98312 | tf_op jit(solution)/shard_map/while/body/eval_jaxpr/ppermute | solution.py:10
  201.4 7.1 %collective-permute-start.8 = (bf16[1,8,64,128]{3,2,1,0:T(8,128)(2,1)S(1)}, bf16[1,8,64,128]{3,2,1,0:T(8,128)(2,1)S(1)}, u32[]{:S(2)}, u32[]{:S(2)}) collective-permute-start(bf16[1,8,64,128]{3,2,1,0:T(8,128)(2,1)S(1)} %get-tuple-element.770), channel_id=1, source_target_pairs={{16,0},{17,1},{18,2},{19,3},{20,4},{21,5},{22,6},{23,7},{24,8},{25... | collective-permute-start | bytes 393224 | tf_op jit(solution)/shard_map/while/body/eval_jaxpr/ppermute | solution.py:10
  205.7 4.0 collective-permute-start.9
  209.8 6.5 %collective-permute-start = (bf16[3,1,1,64,128]{4,3,2,1,0:T(8,128)(2,1)S(1)}, bf16[3,1,1,64,128]{4,3,2,1,0:T(8,128)(2,1)S(1)}, u32[]{:S(2)}, u32[]{:S(2)}) collective-permute-start(bf16[3,1,1,64,128]{4,3,2,1,0:T(8,128)(2,1)S(1)} %get-tuple-element.719), channel_id=1, source_target_pairs={{4,0},{5,1},{6,2},{7,3},{8,4},{9,5},{10,6},{11,7},{12,8},{13,9},{1... | collective-permute-start | bytes 147464 | tf_op jit(solution)/shard_map/while/body/eval_jaxpr/ppermute | solution.py:10
  211.1 6.6 %collective-permute-start.1 = (bf16[3,1,1,64,128]{4,3,2,1,0:T(8,128)(2,1)S(1)}, bf16[3,1,1,64,128]{4,3,2,1,0:T(8,128)(2,1)S(1)}, u32[]{:S(2)}, u32[]{:S(2)}) collective-permute-start(bf16[3,1,1,64,128]{4,3,2,1,0:T(8,128)(2,1)S(1)} %get-tuple-element.720), channel_id=1, source_target_pairs={{0,4},{1,5},{2,6},{3,7},{4,8},{5,9},{6,10},{7,11},{8,12},{9,13},{1... | collective-permute-start | bytes 147464 | tf_op jit(solution)/shard_map/while/body/eval_jaxpr/ppermute | solution.py:10
  225.9 7.4 %collective-permute-start.2 = (bf16[1,1,1,128,128]{4,3,2,1,0:T(8,128)(2,1)}, bf16[1,1,1,128,128]{4,3,2,1,0:T(8,128)(2,1)}, u32[]{:S(2)}, u32[]{:S(2)}) collective-permute-start(bf16[1,1,1,128,128]{4,3,2,1,0:T(8,128)(2,1)} %get-tuple-element.744), channel_id=1, source_target_pairs={{4,0},{5,1},{6,2},{7,3},{8,4},{9,5},{10,6},{11,7},{12,8},{13,9},{1... | collective-permute-start | bytes 98312 | tf_op jit(solution)/shard_map/while/body/eval_jaxpr/ppermute | solution.py:10
  227.2 6.8 %collective-permute-start.3 = (bf16[1,1,1,128,128]{4,3,2,1,0:T(8,128)(2,1)}, bf16[1,1,1,128,128]{4,3,2,1,0:T(8,128)(2,1)}, u32[]{:S(2)}, u32[]{:S(2)}) collective-permute-start(bf16[1,1,1,128,128]{4,3,2,1,0:T(8,128)(2,1)} %get-tuple-element.745), channel_id=1, source_target_pairs={{0,4},{1,5},{2,6},{3,7},{4,8},{5,9},{6,10},{7,11},{8,12},{9,13},{1... | collective-permute-start | bytes 98312 | tf_op jit(solution)/shard_map/while/body/eval_jaxpr/ppermute | solution.py:10
  239.5 6.3 %collective-permute-start.4 = (bf16[3,1,1,64,128]{4,3,2,1,0:T(8,128)(2,1)S(1)}, bf16[3,1,1,64,128]{4,3,2,1,0:T(8,128)(2,1)S(1)}, u32[]{:S(2)}, u32[]{:S(2)}) collective-permute-start(bf16[3,1,1,64,128]{4,3,2,1,0:T(8,128)(2,1)S(1)} %get-tuple-element.754), channel_id=1, source_target_pairs={{4,0},{5,1},{6,2},{7,3},{8,4},{9,5},{10,6},{11,7},{12,8},{13,9},{1... | collective-permute-start | bytes 147464 | tf_op jit(solution)/shard_map/while/body/eval_jaxpr/ppermute | solution.py:10
  240.8 6.6 %collective-permute-start.5 = (bf16[3,1,1,64,128]{4,3,2,1,0:T(8,128)(2,1)S(1)}, bf16[3,1,1,64,128]{4,3,2,1,0:T(8,128)(2,1)S(1)}, u32[]{:S(2)}, u32[]{:S(2)}) collective-permute-start(bf16[3,1,1,64,128]{4,3,2,1,0:T(8,128)(2,1)S(1)} %get-tuple-element.755), channel_id=1, source_target_pairs={{0,4},{1,5},{2,6},{3,7},{4,8},{5,9},{6,10},{7,11},{8,12},{9,13},{1... | collective-permute-start | bytes 147464 | tf_op jit(solution)/shard_map/while/body/eval_jaxpr/ppermute | solution.py:10
  254.8 7.5 %collective-permute-start.6 = (bf16[1,1,1,128,128]{4,3,2,1,0:T(8,128)(2,1)S(1)}, bf16[1,1,1,128,128]{4,3,2,1,0:T(8,128)(2,1)S(1)}, u32[]{:S(2)}, u32[]{:S(2)}) collective-permute-start(bf16[1,1,1,128,128]{4,3,2,1,0:T(8,128)(2,1)S(1)} %get-tuple-element.778), channel_id=1, source_target_pairs={{4,0},{5,1},{6,2},{7,3},{8,4},{9,5},{10,6},{11,7},{12,8},{13,9},{1... | collective-permute-start | bytes 98312 | tf_op jit(solution)/shard_map/while/body/eval_jaxpr/ppermute | solution.py:10
  256.1 6.5 %collective-permute-start.7 = (bf16[1,1,1,128,128]{4,3,2,1,0:T(8,128)(2,1)S(1)}, bf16[1,1,1,128,128]{4,3,2,1,0:T(8,128)(2,1)S(1)}, u32[]{:S(2)}, u32[]{:S(2)}) collective-permute-start(bf16[1,1,1,128,128]{4,3,2,1,0:T(8,128)(2,1)S(1)} %get-tuple-element.779), channel_id=1, source_target_pairs={{0,4},{1,5},{2,6},{3,7},{4,8},{5,9},{6,10},{7,11},{8,12},{9,13},{1... | collective-permute-start | bytes 98312 | tf_op jit(solution)/shard_map/while/body/eval_jaxpr/ppermute | solution.py:10
  261.0 7.1 %collective-permute-start.8 = (bf16[1,8,64,128]{3,2,1,0:T(8,128)(2,1)S(1)}, bf16[1,8,64,128]{3,2,1,0:T(8,128)(2,1)S(1)}, u32[]{:S(2)}, u32[]{:S(2)}) collective-permute-start(bf16[1,8,64,128]{3,2,1,0:T(8,128)(2,1)S(1)} %get-tuple-element.770), channel_id=1, source_target_pairs={{16,0},{17,1},{18,2},{19,3},{20,4},{21,5},{22,6},{23,7},{24,8},{25... | collective-permute-start | bytes 393224 | tf_op jit(solution)/shard_map/while/body/eval_jaxpr/ppermute | solution.py:10
  265.2 4.0 collective-permute-start.9
  269.4 6.5 %collective-permute-start = (bf16[3,1,1,64,128]{4,3,2,1,0:T(8,128)(2,1)S(1)}, bf16[3,1,1,64,128]{4,3,2,1,0:T(8,128)(2,1)S(1)}, u32[]{:S(2)}, u32[]{:S(2)}) collective-permute-start(bf16[3,1,1,64,128]{4,3,2,1,0:T(8,128)(2,1)S(1)} %get-tuple-element.719), channel_id=1, source_target_pairs={{4,0},{5,1},{6,2},{7,3},{8,4},{9,5},{10,6},{11,7},{12,8},{13,9},{1... | collective-permute-start | bytes 147464 | tf_op jit(solution)/shard_map/while/body/eval_jaxpr/ppermute | solution.py:10
  270.7 6.6 %collective-permute-start.1 = (bf16[3,1,1,64,128]{4,3,2,1,0:T(8,128)(2,1)S(1)}, bf16[3,1,1,64,128]{4,3,2,1,0:T(8,128)(2,1)S(1)}, u32[]{:S(2)}, u32[]{:S(2)}) collective-permute-start(bf16[3,1,1,64,128]{4,3,2,1,0:T(8,128)(2,1)S(1)} %get-tuple-element.720), channel_id=1, source_target_pairs={{0,4},{1,5},{2,6},{3,7},{4,8},{5,9},{6,10},{7,11},{8,12},{9,13},{1... | collective-permute-start | bytes 147464 | tf_op jit(solution)/shard_map/while/body/eval_jaxpr/ppermute | solution.py:10
  285.5 7.4 %collective-permute-start.2 = (bf16[1,1,1,128,128]{4,3,2,1,0:T(8,128)(2,1)}, bf16[1,1,1,128,128]{4,3,2,1,0:T(8,128)(2,1)}, u32[]{:S(2)}, u32[]{:S(2)}) collective-permute-start(bf16[1,1,1,128,128]{4,3,2,1,0:T(8,128)(2,1)} %get-tuple-element.744), channel_id=1, source_target_pairs={{4,0},{5,1},{6,2},{7,3},{8,4},{9,5},{10,6},{11,7},{12,8},{13,9},{1... | collective-permute-start | bytes 98312 | tf_op jit(solution)/shard_map/while/body/eval_jaxpr/ppermute | solution.py:10
  286.8 6.8 %collective-permute-start.3 = (bf16[1,1,1,128,128]{4,3,2,1,0:T(8,128)(2,1)}, bf16[1,1,1,128,128]{4,3,2,1,0:T(8,128)(2,1)}, u32[]{:S(2)}, u32[]{:S(2)}) collective-permute-start(bf16[1,1,1,128,128]{4,3,2,1,0:T(8,128)(2,1)} %get-tuple-element.745), channel_id=1, source_target_pairs={{0,4},{1,5},{2,6},{3,7},{4,8},{5,9},{6,10},{7,11},{8,12},{9,13},{1... | collective-permute-start | bytes 98312 | tf_op jit(solution)/shard_map/while/body/eval_jaxpr/ppermute | solution.py:10
  299.1 6.3 %collective-permute-start.4 = (bf16[3,1,1,64,128]{4,3,2,1,0:T(8,128)(2,1)S(1)}, bf16[3,1,1,64,128]{4,3,2,1,0:T(8,128)(2,1)S(1)}, u32[]{:S(2)}, u32[]{:S(2)}) collective-permute-start(bf16[3,1,1,64,128]{4,3,2,1,0:T(8,128)(2,1)S(1)} %get-tuple-element.754), channel_id=1, source_target_pairs={{4,0},{5,1},{6,2},{7,3},{8,4},{9,5},{10,6},{11,7},{12,8},{13,9},{1... | collective-permute-start | bytes 147464 | tf_op jit(solution)/shard_map/while/body/eval_jaxpr/ppermute | solution.py:10
  300.4 6.6 %collective-permute-start.5 = (bf16[3,1,1,64,128]{4,3,2,1,0:T(8,128)(2,1)S(1)}, bf16[3,1,1,64,128]{4,3,2,1,0:T(8,128)(2,1)S(1)}, u32[]{:S(2)}, u32[]{:S(2)}) collective-permute-start(bf16[3,1,1,64,128]{4,3,2,1,0:T(8,128)(2,1)S(1)} %get-tuple-element.755), channel_id=1, source_target_pairs={{0,4},{1,5},{2,6},{3,7},{4,8},{5,9},{6,10},{7,11},{8,12},{9,13},{1... | collective-permute-start | bytes 147464 | tf_op jit(solution)/shard_map/while/body/eval_jaxpr/ppermute | solution.py:10
  314.4 7.5 %collective-permute-start.6 = (bf16[1,1,1,128,128]{4,3,2,1,0:T(8,128)(2,1)S(1)}, bf16[1,1,1,128,128]{4,3,2,1,0:T(8,128)(2,1)S(1)}, u32[]{:S(2)}, u32[]{:S(2)}) collective-permute-start(bf16[1,1,1,128,128]{4,3,2,1,0:T(8,128)(2,1)S(1)} %get-tuple-element.778), channel_id=1, source_target_pairs={{4,0},{5,1},{6,2},{7,3},{8,4},{9,5},{10,6},{11,7},{12,8},{13,9},{1... | collective-permute-start | bytes 98312 | tf_op jit(solution)/shard_map/while/body/eval_jaxpr/ppermute | solution.py:10
  315.7 6.5 %collective-permute-start.7 = (bf16[1,1,1,128,128]{4,3,2,1,0:T(8,128)(2,1)S(1)}, bf16[1,1,1,128,128]{4,3,2,1,0:T(8,128)(2,1)S(1)}, u32[]{:S(2)}, u32[]{:S(2)}) collective-permute-start(bf16[1,1,1,128,128]{4,3,2,1,0:T(8,128)(2,1)S(1)} %get-tuple-element.779), channel_id=1, source_target_pairs={{0,4},{1,5},{2,6},{3,7},{4,8},{5,9},{6,10},{7,11},{8,12},{9,13},{1... | collective-permute-start | bytes 98312 | tf_op jit(solution)/shard_map/while/body/eval_jaxpr/ppermute | solution.py:10
  320.6 7.1 %collective-permute-start.8 = (bf16[1,8,64,128]{3,2,1,0:T(8,128)(2,1)S(1)}, bf16[1,8,64,128]{3,2,1,0:T(8,128)(2,1)S(1)}, u32[]{:S(2)}, u32[]{:S(2)}) collective-permute-start(bf16[1,8,64,128]{3,2,1,0:T(8,128)(2,1)S(1)} %get-tuple-element.770), channel_id=1, source_target_pairs={{16,0},{17,1},{18,2},{19,3},{20,4},{21,5},{22,6},{23,7},{24,8},{25... | collective-permute-start | bytes 393224 | tf_op jit(solution)/shard_map/while/body/eval_jaxpr/ppermute | solution.py:10
  324.8 4.0 collective-permute-start.9
  329.0 6.5 %collective-permute-start = (bf16[3,1,1,64,128]{4,3,2,1,0:T(8,128)(2,1)S(1)}, bf16[3,1,1,64,128]{4,3,2,1,0:T(8,128)(2,1)S(1)}, u32[]{:S(2)}, u32[]{:S(2)}) collective-permute-start(bf16[3,1,1,64,128]{4,3,2,1,0:T(8,128)(2,1)S(1)} %get-tuple-element.719), channel_id=1, source_target_pairs={{4,0},{5,1},{6,2},{7,3},{8,4},{9,5},{10,6},{11,7},{12,8},{13,9},{1... | collective-permute-start | bytes 147464 | tf_op jit(solution)/shard_map/while/body/eval_jaxpr/ppermute | solution.py:10
  330.3 6.6 %collective-permute-start.1 = (bf16[3,1,1,64,128]{4,3,2,1,0:T(8,128)(2,1)S(1)}, bf16[3,1,1,64,128]{4,3,2,1,0:T(8,128)(2,1)S(1)}, u32[]{:S(2)}, u32[]{:S(2)}) collective-permute-start(bf16[3,1,1,64,128]{4,3,2,1,0:T(8,128)(2,1)S(1)} %get-tuple-element.720), channel_id=1, source_target_pairs={{0,4},{1,5},{2,6},{3,7},{4,8},{5,9},{6,10},{7,11},{8,12},{9,13},{1... | collective-permute-start | bytes 147464 | tf_op jit(solution)/shard_map/while/body/eval_jaxpr/ppermute | solution.py:10
  345.1 7.4 %collective-permute-start.2 = (bf16[1,1,1,128,128]{4,3,2,1,0:T(8,128)(2,1)}, bf16[1,1,1,128,128]{4,3,2,1,0:T(8,128)(2,1)}, u32[]{:S(2)}, u32[]{:S(2)}) collective-permute-start(bf16[1,1,1,128,128]{4,3,2,1,0:T(8,128)(2,1)} %get-tuple-element.744), channel_id=1, source_target_pairs={{4,0},{5,1},{6,2},{7,3},{8,4},{9,5},{10,6},{11,7},{12,8},{13,9},{1... | collective-permute-start | bytes 98312 | tf_op jit(solution)/shard_map/while/body/eval_jaxpr/ppermute | solution.py:10
  346.4 6.8 %collective-permute-start.3 = (bf16[1,1,1,128,128]{4,3,2,1,0:T(8,128)(2,1)}, bf16[1,1,1,128,128]{4,3,2,1,0:T(8,128)(2,1)}, u32[]{:S(2)}, u32[]{:S(2)}) collective-permute-start(bf16[1,1,1,128,128]{4,3,2,1,0:T(8,128)(2,1)} %get-tuple-element.745), channel_id=1, source_target_pairs={{0,4},{1,5},{2,6},{3,7},{4,8},{5,9},{6,10},{7,11},{8,12},{9,13},{1... | collective-permute-start | bytes 98312 | tf_op jit(solution)/shard_map/while/body/eval_jaxpr/ppermute | solution.py:10
  358.6 6.3 %collective-permute-start.4 = (bf16[3,1,1,64,128]{4,3,2,1,0:T(8,128)(2,1)S(1)}, bf16[3,1,1,64,128]{4,3,2,1,0:T(8,128)(2,1)S(1)}, u32[]{:S(2)}, u32[]{:S(2)}) collective-permute-start(bf16[3,1,1,64,128]{4,3,2,1,0:T(8,128)(2,1)S(1)} %get-tuple-element.754), channel_id=1, source_target_pairs={{4,0},{5,1},{6,2},{7,3},{8,4},{9,5},{10,6},{11,7},{12,8},{13,9},{1... | collective-permute-start | bytes 147464 | tf_op jit(solution)/shard_map/while/body/eval_jaxpr/ppermute | solution.py:10
  359.9 6.6 %collective-permute-start.5 = (bf16[3,1,1,64,128]{4,3,2,1,0:T(8,128)(2,1)S(1)}, bf16[3,1,1,64,128]{4,3,2,1,0:T(8,128)(2,1)S(1)}, u32[]{:S(2)}, u32[]{:S(2)}) collective-permute-start(bf16[3,1,1,64,128]{4,3,2,1,0:T(8,128)(2,1)S(1)} %get-tuple-element.755), channel_id=1, source_target_pairs={{0,4},{1,5},{2,6},{3,7},{4,8},{5,9},{6,10},{7,11},{8,12},{9,13},{1... | collective-permute-start | bytes 147464 | tf_op jit(solution)/shard_map/while/body/eval_jaxpr/ppermute | solution.py:10
  374.0 7.5 %collective-permute-start.6 = (bf16[1,1,1,128,128]{4,3,2,1,0:T(8,128)(2,1)S(1)}, bf16[1,1,1,128,128]{4,3,2,1,0:T(8,128)(2,1)S(1)}, u32[]{:S(2)}, u32[]{:S(2)}) collective-permute-start(bf16[1,1,1,128,128]{4,3,2,1,0:T(8,128)(2,1)S(1)} %get-tuple-element.778), channel_id=1, source_target_pairs={{4,0},{5,1},{6,2},{7,3},{8,4},{9,5},{10,6},{11,7},{12,8},{13,9},{1... | collective-permute-start | bytes 98312 | tf_op jit(solution)/shard_map/while/body/eval_jaxpr/ppermute | solution.py:10
  375.3 6.5 %collective-permute-start.7 = (bf16[1,1,1,128,128]{4,3,2,1,0:T(8,128)(2,1)S(1)}, bf16[1,1,1,128,128]{4,3,2,1,0:T(8,128)(2,1)S(1)}, u32[]{:S(2)}, u32[]{:S(2)}) collective-permute-start(bf16[1,1,1,128,128]{4,3,2,1,0:T(8,128)(2,1)S(1)} %get-tuple-element.779), channel_id=1, source_target_pairs={{0,4},{1,5},{2,6},{3,7},{4,8},{5,9},{6,10},{7,11},{8,12},{9,13},{1... | collective-permute-start | bytes 98312 | tf_op jit(solution)/shard_map/while/body/eval_jaxpr/ppermute | solution.py:10
  380.2 7.1 %collective-permute-start.8 = (bf16[1,8,64,128]{3,2,1,0:T(8,128)(2,1)S(1)}, bf16[1,8,64,128]{3,2,1,0:T(8,128)(2,1)S(1)}, u32[]{:S(2)}, u32[]{:S(2)}) collective-permute-start(bf16[1,8,64,128]{3,2,1,0:T(8,128)(2,1)S(1)} %get-tuple-element.770), channel_id=1, source_target_pairs={{16,0},{17,1},{18,2},{19,3},{20,4},{21,5},{22,6},{23,7},{24,8},{25... | collective-permute-start | bytes 393224 | tf_op jit(solution)/shard_map/while/body/eval_jaxpr/ppermute | solution.py:10
  384.4 4.0 collective-permute-start.9
  389.4 10.1 %collective-permute-start.12 = (bf16[5,1,4,64,128]{4,3,2,1,0:T(8,128)(2,1)S(1)}, bf16[5,1,4,64,128]{4,3,2,1,0:T(8,128)(2,1)S(1)}, u32[]{:S(2)}, u32[]{:S(2)}) collective-permute-start(bf16[5,1,4,64,128]{4,3,2,1,0:T(8,128)(2,1)S(1)} %get-tuple-element.556), channel_id=1, source_target_pairs={{0,2},{2,0},{1,3},{3,1},{4,6},{6,4},{5,7},{7,5},{8,10},{10,8},{9,1... | collective-permute-start | bytes 983048 | tf_op jit(solution)/shard_map/ppermute | solution.py:20
  399.6 9.2 %collective-permute-start.13 = (bf16[5,2,2,64,128]{4,3,2,1,0:T(8,128)(2,1)S(1)}, bf16[5,2,2,64,128]{4,3,2,1,0:T(8,128)(2,1)S(1)}, u32[]{:S(2)}, u32[]{:S(2)}) collective-permute-start(bf16[5,2,2,64,128]{4,3,2,1,0:T(8,128)(2,1)S(1)} %get-tuple-element.554), channel_id=1, source_target_pairs={{0,1},{1,0},{2,3},{3,2},{4,5},{5,4},{6,7},{7,6},{8,9},{9,8},{10,11... | collective-permute-start | bytes 983048 | tf_op jit(solution)/shard_map/ppermute | solution.py:20
  (109 other events, 397.0 us)
where the time goes:
time: 415 us; the launch traced here: 411 us
  starting transfers between devices  183 us (44%)
  local copies, waits for them, and re-layouts  90.3 us (22%)
  waiting for transfers between devices  71.2 us (17%)
  matrix products  37 us (9%)
  other arithmetic  22.7 us (5%)
  loops' own time  5.96 us (1%)
    ppermute x60, starting transfers between devices, shifted(): return lax.ppermute(block, axis, route)  175 us
    while x600, local copies, waits for them, and re-layouts  57.1 us
    ppermute x4, waiting for transfers between devices, partner(): return lax.ppermute(block, axis, route)  39.4 us
    ppermute x60, waiting for transfers between devices, shifted(): return lax.ppermute(block, axis, route)  31.8 us
    dot_general x48, matrix products, convolve(): jnp.einsum('ko,brkw->brow', weight, taps, preferred_element_type=jnp.floa...  30.5 us
    slice x48, local copies, waits for them, and re-layouts, shifted_taps(): pieces.append(jnp.concatenate([row_band[..., 1:], zero_column], axis=-1))  13.7 us
    convert_element_type x12, other arithmetic, gate_math(): cell_new = (jax.nn.sigmoid(parts_x[1] + parts_h[1] + 1.0) * cell_prev.ast...  9.2 us
  transfers between devices with their start and end apart: 64, of which 46 were waited for; matrix products, arithmetic and copies ran while one was open for 4% of the time, Pallas kernels for 0%

commit v1 on v0

v1 whole, which is shorter than its diff:
```python
import functools

import jax
import jax.numpy as jnp
from jax import lax
from jax.experimental import pallas as pl
from jax.experimental.pallas import tpu as pltpu
from jax.sharding import PartitionSpec as P

MESH = pl.DeviceIdType.MESH
F32 = jnp.float32
BF16 = jnp.bfloat16


def sig(x):
    return 0.5 * jnp.tanh(0.5 * x) + 0.5


def kernel(
    rows_total, layers, steps,
    frames, hidden, cell, memory, weights,
    hid_out, cell_out, mem_out,
    taps, wbuf, land_h, land_c, land_cs, land_m, land_f,
    h_send, h_land, m_send, m_land, cell_state, mem_state, cell_last, acc_h, acc_m, acc_o,
    r_w, s_w, r_h, s_h, s_hc, r_c, r_cs, s_c, s_cc, r_m, s_m, r_f, s_f,
    r_hl, s_hl, r_ml, s_ml, r_out, s_out, l_out,
):
    core, row = lax.axis_index("layer"), lax.axis_index("rows")
    other = 1 - core
    local_layers, seqs_all, band, ch, width = hidden.shape
    cores = layers // local_layers
    seqs = seqs_all // cores
    cells = layers * steps
    tap = 3 * ch
    span = band + 4
    t_frame, t_mem, t_cell = 0, layers + 1, layers + 2
    has_up, has_down = row > 0, row < rows_total - 1
    up, down = lax.rem(row + rows_total - 1, rows_total), lax.rem(row + 1, rows_total)

    def to(c, r):
        return {"layer": c, "rows": r}

    def remote(src, dst, send, recv, c, r):
        return pltpu.make_async_remote_copy(
            src_ref=src, dst_ref=dst, send_sem=send, recv_sem=recv,
            device_id=to(c, r), device_id_type=MESH,
        )

    def arrived(dst, sem):
        pltpu.make_async_copy(dst, dst, sem).wait()

    lane = lax.broadcasted_iota(jnp.int32, (ch, width), 1)

    def put_taps(index, r, s, value):
        wide = value.astype(F32)
        left = jnp.where(lane == 0, 0.0, pltpu.roll(wide, 1, 1)).astype(BF16)
        right = jnp.where(lane == width - 1, 0.0, pltpu.roll(wide, width - 1, 1)).astype(BF16)
        cols = slice(s * width, (s + 1) * width)
        taps[index, r * tap : r * tap + ch, cols] = left
        taps[index, r * tap + ch : r * tap + 2 * ch, cols] = value.astype(BF16)
        taps[index, r * tap + 2 * ch : (r + 1) * tap, cols] = right

    def window(index, r):
        return taps[index, (r - 1) * tap : (r + 2) * tap, :]

    barrier = pltpu.get_barrier_semaphore()
    pl.semaphore_signal(barrier, inc=1, device_id=to(other, row), device_id_type=MESH)

    @pl.when(has_up)
    def _():
        for c in range(cores):
            pl.semaphore_signal(barrier, inc=1, device_id=to(c, up), device_id_type=MESH)

    @pl.when(has_down)
    def _():
        for c in range(cores):
            pl.semaphore_signal(barrier, inc=1, device_id=to(c, down), device_id_type=MESH)

    edge = 2 * tap
    for index in range(layers + 3):
        taps[index, :edge, :] = jnp.zeros((edge, taps.shape[2]), BF16)
        taps[index, (span - 2) * tap :, :] = jnp.zeros((edge, taps.shape[2]), BF16)
    mem_state[0] = jnp.zeros(mem_state.shape[1:], BF16)
    mem_state[band + 1] = jnp.zeros(mem_state.shape[1:], BF16)
    for layer in range(layers):
        cell_state[layer, 0] = jnp.zeros(mem_state.shape[1:], BF16)
        cell_state[layer, band + 1] = jnp.zeros(mem_state.shape[1:], BF16)

    near = has_up.astype(jnp.int32) + has_down.astype(jnp.int32)
    pl.semaphore_wait(barrier, 1 + cores * near)

    mine = pl.ds(core * seqs, seqs)
    theirs = pl.ds(other * seqs, seqs)

    def center_copies(j):
        layer = core * local_layers + j
        local = [
            pltpu.make_async_copy(weights.at[j], wbuf.at[layer], r_w.at[layer]),
            pltpu.make_async_copy(hidden.at[j, mine], land_h.at[layer, 1], r_h.at[layer, 1]),
            pltpu.make_async_copy(cell.at[j, mine], land_c.at[layer], r_c.at[layer]),
        ]
        far = [
            remote(weights.at[j], wbuf.at[layer], s_w.at[j], r_w.at[layer], other, row),
            remote(hidden.at[j, theirs], land_h.at[layer, 1], s_hc.at[j], r_h.at[layer, 1], other, row),
            remote(cell.at[j, theirs], land_c.at[layer], s_cc.at[j], r_c.at[layer], other, row),
        ]
        return local, far

    def halo_copies(j, side):
        layer = core * local_layers + j
        target = down if side == 0 else up
        edge_row = band - 1 if side == 0 else 0
        result = []
        for c in range(cores):
            part = pl.ds(c * seqs, seqs)
            result.append(remote(hidden.at[j, part], land_h.at[layer, 2 * side],
                                 s_h.at[j, c, side], r_h.at[layer, 2 * side], c, target))
            result.append(remote(cell.at[j, part, edge_row], land_cs.at[layer, side],
                                 s_c.at[j, c, side], r_cs.at[layer, side], c, target))
        return result

    def frame_copy(t, side):
        target = down if side == 0 else up
        return remote(frames.at[t, mine], land_f.at[t, side], s_f.at[t, side], r_f.at[t, side], core, target)

    def memory_copy(side):
        target = down if side == 0 else up
        return remote(memory.at[mine], land_m.at[side], s_m.at[side], r_m.at[side], core, target)

    sides = ((0, has_down), (1, has_up))
    from_sides = ((0, has_up), (1, has_down))

    for j in range(local_layers):
        local, far = center_copies(j)
        for copy in far + local:
            copy.start()
        for side, there in sides:

            @pl.when(there)
            def _():
                if j == 0:
                    memory_copy(side).start()
                    frame_copy(0, side).start()
                for copy in halo_copies(j, side):
                    copy.start()

    for t in range(1, steps):
        for side, there in sides:

            @pl.when(there)
            def _():
                frame_copy(t, side).start()

    for s in range(seqs):
        cols = slice(s * width, (s + 1) * width)
        for r in range(band):
            value = memory[core * seqs + s, r]
            put_taps(t_mem, 2 + r, s, value)
            mem_state[1 + r, :, cols] = value
    for side, there in from_sides:

        @pl.when(there)
        def _():
            arrived(land_m.at[side], r_m.at[side])
            first = 0 if side == 0 else span - 2
            for s in range(seqs):
                cols = slice(s * width, (s + 1) * width)
                for r in range(2):
                    put_taps(t_mem, first + r, s, land_m[side, s, r])
                if side == 0:
                    mem_state[0, :, cols] = land_m[side, s, band - 1]
                else:
                    mem_state[band + 1, :, cols] = land_m[side, s, 0]

    def h_copy(k, side):
        target = down if side == 0 else up
        return remote(h_send.at[k], h_land.at[k, side], s_hl.at[k, side], r_hl.at[k, side], core, target)

    def m_copy(k, side):
        target = down if side == 0 else up
        edge_row = 0 if side == 0 else band - 1
        return remote(m_send.at[k, :, edge_row], m_land.at[k, side], s_ml.at[k, side], r_ml.at[k, side], core, target)

    def step(k, carry):
        layer = lax.rem(k, layers)
        t = lax.div(k, layers)
        prev = lax.rem(k + cells - 1, cells)
        before = lax.rem(k + layers - 1, layers)

        @pl.when(k < layers)
        def _():
            arrived(wbuf.at[layer], r_w.at[layer])
            arrived(land_h.at[layer, 1], r_h.at[layer, 1])
            arrived(land_c.at[layer], r_c.at[layer])
            for s in range(seqs):
                cols = slice(s * width, (s + 1) * width)
                for r in range(band):
                    put_taps(layer + 1, 2 + r, s, land_h[layer, 1, s, r])
                    cell_state[layer, 1 + r, :, cols] = land_c[layer, s, r]
            for side, there in from_sides:

                @pl.when(there)
                def _():
                    arrived(land_h.at[layer, 2 * side], r_h.at[layer, 2 * side])
                    arrived(land_cs.at[layer, side], r_cs.at[layer, side])
                    first = 0 if side == 0 else span - 2
                    for s in range(seqs):
                        cols = slice(s * width, (s + 1) * width)
                        for r in range(2):
                            put_taps(layer + 1, first + r, s, land_h[layer, 2 * side, s, r])
                        cell_state[layer, 0 if side == 0 else band + 1, :, cols] = land_cs[layer, side, s]

        @pl.when(layer == 0)
        def _():
            for s in range(seqs):
                for r in range(band):
                    put_taps(t_frame, 2 + r, s, frames[t, core * seqs + s, r])
            for side, there in from_sides:

                @pl.when(there)
                def _():
                    arrived(land_f.at[t, side], r_f.at[t, side])
                    first = 0 if side == 0 else span - 2
                    for s in range(seqs):
                        for r in range(2):
                            put_taps(t_frame, first + r, s, land_f[t, side, s, r])

        w_h = wbuf[layer, 7 * ch : 11 * ch, :]
        for r in range(1, band + 3):
            acc_h[r - 1] = jnp.dot(w_h, window(layer + 1, r), preferred_element_type=F32)

        for side, there in from_sides:

            @pl.when(there)
            def _():
                @pl.when(k > 0)
                def _():
                    arrived(m_land.at[prev, side], r_ml.at[prev, side])
                    for s in range(seqs):
                        put_taps(t_mem, 0 if side == 0 else span - 1, s, m_land[prev, side, s])

        w_m = wbuf[layer, 11 * ch : 14 * ch, :]
        for r in range(1, band + 3):
            acc_m[r - 1] = jnp.dot(w_m, window(t_mem, r), preferred_element_type=F32)

        for side, there in from_sides:

            @pl.when(there)
            def _():
                @pl.when(k > 0)
                def _():
                    arrived(h_land.at[prev, side], r_hl.at[prev, side])
                    first = 0 if side == 0 else span - 2
                    for s in range(seqs):
                        for r in range(2):
                            put_taps(before + 1, first + r, s, h_land[prev, side, s, r])

        w_x = wbuf[layer, : 7 * ch, :]
        for r in range(1, band + 3):
            a = jnp.dot(w_x, window(layer, r), preferred_element_type=F32)
            q = r - 1
            part = lambda n: a[n * ch : (n + 1) * ch]
            of_h = lambda n: acc_h[q, n * ch : (n + 1) * ch, :]
            of_m = lambda n: acc_m[q, n * ch : (n + 1) * ch, :]
            c_new = sig(part(1) + of_h(1) + 1.0) * cell_state[layer, q].astype(F32) + sig(
                part(0) + of_h(0)
            ) * jnp.tanh(part(2) + of_h(2))
            m_new = sig(part(4) + of_m(1) + 1.0) * mem_state[q].astype(F32) + sig(
                part(3) + of_m(0)
            ) * jnp.tanh(part(5) + of_m(2))
            if r == 1:
                c_new = jnp.where(has_up, c_new, 0.0)
                m_new = jnp.where(has_up, m_new, 0.0)
            if r == band + 2:
                c_new = jnp.where(has_down, c_new, 0.0)
                m_new = jnp.where(has_down, m_new, 0.0)
            c_new = c_new.astype(BF16)
            m_new = m_new.astype(BF16)
            cell_state[layer, q] = c_new
            mem_state[q] = m_new
            own = 2 <= r < band + 2
            for s in range(seqs):
                cols = slice(s * width, (s + 1) * width)
                put_taps(t_cell, r, s, c_new[:, cols])
                put_taps(t_mem, r, s, m_new[:, cols])
                if own:
                    cell_last[layer, s, r - 2] = c_new[:, cols]
                    m_send[k, s, r - 2] = m_new[:, cols]
            if own:
                acc_o[r - 2] = part(6) + of_h(3)

        for side, there in sides:

            @pl.when(there)
            def _():
                @pl.when(k < cells - 1)
                def _():
                    m_copy(k, side).start()

        w_c = wbuf[layer, 14 * ch : 16 * ch, :]
        w_n = wbuf[layer, 16 * ch : 18 * ch, :]
        for r in range(2, band + 2):
            both = jnp.dot(w_c, window(t_cell, r), preferred_element_type=F32)
            both = both + jnp.dot(w_n, window(t_mem, r), preferred_element_type=F32)
            h_new = (sig(acc_o[r - 2] + both[:ch]) * jnp.tanh(both[ch:])).astype(BF16)
            for s in range(seqs):
                h_send[k, s, r - 2] = h_new[:, s * width : (s + 1) * width]

        for side, there in sides:

            @pl.when(there)
            def _():
                @pl.when(k < cells - 1)
                def _():
                    h_copy(k, side).start()

        for s in range(seqs):
            for r in range(band):
                put_taps(layer + 1, 2 + r, s, h_send[k, s, r])
        return carry

    lax.fori_loop(0, cells, step, 0)

    last = cells - layers
    far_layers = pl.ds(last + other * local_layers, local_layers)
    own_layers = pl.ds(last + core * local_layers, local_layers)
    far_out = [
        remote(h_send.at[far_layers], hid_out.at[:, mine], s_out.at[0], r_out.at[0], other, row),
        remote(cell_last.at[pl.ds(other * local_layers, local_layers)], cell_out.at[:, mine],
               s_out.at[1], r_out.at[1], other, row),
        remote(m_send.at[last + other * local_layers + local_layers - 1], mem_out.at[0, mine],
               s_out.at[2], r_out.at[2], other, row),
    ]
    own_out = [
        pltpu.make_async_copy(h_send.at[own_layers], hid_out.at[:, mine], l_out.at[0]),
        pltpu.make_async_copy(cell_last.at[pl.ds(core * local_layers, local_layers)],
                              cell_out.at[:, mine], l_out.at[1]),
        pltpu.make_async_copy(m_send.at[last + core * local_layers + local_layers - 1],
                              mem_out.at[0, mine], l_out.at[2]),
    ]
    for copy in far_out + own_out:
        copy.start()

    for j in range(local_layers):
        for copy in center_copies(j)[1]:
            copy.wait_send()
    for side, there in sides:

        @pl.when(there)
        def _():
            memory_copy(side).wait_send()
            for t in range(steps):
                frame_copy(t, side).wait_send()
            for j in range(local_layers):
                for copy in halo_copies(j, side):
                    copy.wait_send()

            def drain(k, carry):
                h_copy(k, side).wait_send()
                m_copy(k, side).wait_send()
                return carry

            lax.fori_loop(0, cells - 1, drain, 0)

    for copy in own_out:
        copy.wait()
    for copy in far_out:
        copy.wait_send()
    arrived(hid_out.at[:, theirs], r_out.at[0])
    arrived(cell_out.at[:, theirs], r_out.at[1])
    arrived(mem_out.at[0, theirs], r_out.at[2])


def pack(w_x, w_h, w_m, w_o, w_last):
    layers, depth, _ = w_x.shape
    ch = w_last.shape[2]
    taps = depth // ch
    split = w_o.reshape(layers, taps, 2, ch, ch)
    mix = w_last.reshape(layers, 2, ch, ch)
    pieces = [w_x, w_h, w_m]
    for half in range(2):
        pieces.append(split[:, :, half].reshape(layers, depth, ch))
        middle = (taps // 2) * ch
        pieces.append(jnp.pad(mix[:, half], ((0, 0), (middle, depth - middle - ch), (0, 0))))
    return jnp.concatenate(pieces, axis=2).transpose(0, 2, 1)


def on_device(rows_total, cores, frames, hidden_in, cell_in, memory_in, w_x, w_h, w_m, w_o, w_last):
    steps = frames.shape[0]
    local_layers, seqs_all, band, ch, width = hidden_in.shape
    layers = local_layers * cores
    seqs = seqs_all // cores
    cells = layers * steps
    lanes = seqs * width
    weights = pack(w_x, w_h, w_m, w_o, w_last)
    block = (seqs, band, ch, width)
    dma = pltpu.SemaphoreType.DMA
    vm = lambda *shape: pltpu.VMEM(shape, BF16)
    vf = lambda *shape: pltpu.VMEM(shape, F32)
    in_vmem = pl.BlockSpec(memory_space=pltpu.VMEM)
    return pl.pallas_call(
        functools.partial(kernel, rows_total, layers, steps),
        out_shape=(
            jax.ShapeDtypeStruct(hidden_in.shape, BF16),
            jax.ShapeDtypeStruct(cell_in.shape, BF16),
            jax.ShapeDtypeStruct((1,) + memory_in.shape, BF16),
        ),
        in_specs=[in_vmem] * 4 + [pl.BlockSpec(memory_space=pl.ANY)],
        out_specs=(in_vmem,) * 3,
        scratch_shapes=[
            vm(layers + 3, (band + 4) * 3 * ch, lanes),
            vm(layers, *weights.shape[1:]),
            vm(layers, 3, *block),
            vm(layers, *block),
            vm(layers, 2, seqs, ch, width),
            vm(2, *block),
            vm(steps, 2, *block),
            vm(cells, *block),
            vm(cells, 2, *block),
            vm(cells, *block),
            vm(cells, 2, seqs, ch, width),
            vm(layers, band + 2, ch, lanes),
            vm(band + 2, ch, lanes),
            vm(layers, *block),
            vf(band + 2, 4 * ch, lanes),
            vf(band + 2, 3 * ch, lanes),
            vf(band, ch, lanes),
            dma((layers,)), dma((local_layers,)),
            dma((layers, 3)), dma((local_layers, cores, 2)), dma((local_layers,)),
            dma((layers,)), dma((layers, 2)), dma((local_layers, cores, 2)), dma((local_layers,)),
            dma((2,)), dma((2,)),
            dma((steps, 2)), dma((steps, 2)),
            dma((cells, 2)), dma((cells, 2)),
            dma((cells, 2)), dma((cells, 2)),
            dma((3,)), dma((3,)), dma((3,)),
        ],
        compiler_params=pltpu.CompilerParams(
            collective_id=0, has_side_effects=True, vmem_limit_bytes=48 * 1024 * 1024
        ),
    )(frames, hidden_in, cell_in, memory_in, weights)


def solution(mesh):
    return jax.shard_map(
        functools.partial(on_device, mesh.shape["rows"], mesh.shape["layer"]),
        mesh=mesh,
        in_specs=(
            P(None, None, "rows", None, None),
            P("layer", None, "rows", None, None),
            P("layer", None, "rows", None, None),
            P(None, "rows", None, None),
            P("layer", None, None),
            P("layer", None, None),
            P("layer", None, None),
            P("layer", None, None),
            P("layer", None, None),
        ),
        out_specs=(
            P("layer", None, "rows", None, None),
            P("layer", None, "rows", None, None),
            P("layer", None, "rows", None, None),
        ),
        check_vma=False,
    )
```

time: 415 us -> 137 us (0.33)
  starting transfers between devices: 183 us -> 0 us
  Pallas kernels: 0 us -> 110 us
  waiting for transfers between devices: 71.2 us -> 0 us
  local copies, waits for them, and re-layouts: 90.3 us -> 24.6 us
  matrix products: 37 us -> 0 us
  other arithmetic: 22.7 us -> 0 us
  loops' own time: 5.96 us -> 0 us
    ppermute x64 -> x0, starting transfers between devices: 183 us -> none  [the longest x60 175 us: shifted(): return lax.ppermute(block, axis, route)]
    pallas_call x0 -> x1, Pallas kernels: none -> 110 us  [on_device(): pl.pallas_call(functools.partial(kernel, rows_total, layers, steps), out_...]
    ppermute x64 -> x0, waiting for transfers between devices: 71.2 us -> none  [the longest x4 39.4 us: partner(): return lax.ppermute(block, axis, route)]
    while x600 -> x0, local copies, waits for them, and re-layouts: 57.1 us -> none
    dot_general x60 -> x0, matrix products: 37 us -> none  [the longest x48 30.5 us: convolve(): jnp.einsum('ko,brkw->brow', weight, taps, preferred_element_type=jnp.floa...]
    slice x65 -> x2, local copies, waits for them, and re-layouts: 19.6 us -> 3.47 us  [the longest x1 3.37 us: pack(): pieces.append(split[:, :, half].reshape(layers, depth, ch))]
    unnamed x4 -> x22, local copies, waits for them, and re-layouts: 0.94 us -> 14.5 us
    dynamic_slice x18 -> x0, local copies, waits for them, and re-layouts: 9.48 us -> none  [the longest x12 5.54 us: advance(): hidden_prev = lax.dynamic_slice(hidden_loc, corner, block_shape)[0]]
  transfers between devices with their start and end apart: 64 -> 0, of which waited for: 46 -> 0; matrix products, arithmetic and copies ran while one was open for 4% -> 0% of each run, Pallas kernels for 0% -> 0%
where the time goes in v1:
time: 137 us; the launch traced here: 136 us
  Pallas kernels  110 us (80%)
  local copies, waits for them, and re-layouts  24.6 us (18%)
    pallas_call x1, Pallas kernels, on_device(): pl.pallas_call(functools.partial(kernel, rows_total, layers, steps), out_...  110 us
    unnamed x22, local copies, waits for them, and re-layouts  14.5 us
    another operation x2, local copies, waits for them, and re-layouts, pack(): pieces.append(split[:, :, half].reshape(layers, depth, ch))  3.56 us
    slice x1, local copies, waits for them, and re-layouts, pack(): pieces.append(split[:, :, half].reshape(layers, depth, ch))  3.37 us

profile of v1, /device:TPU:0, one launch (start us, length us, event | category | flops | bytes accessed | tf_op | source)
XLA Modules:
  0.0 135.7 jit_solution(12835377517942754409)
XLA Ops:
  0.6 0.0 copy-start.4
  0.6 1.4 %constant_dynamic-update-slice_fusion.4 = bf16[2,576,1152]{1,2,0:T(8,128)(2,1)S(1)} fusion(bf16[2,576,448]{1,2,0:T(8,128)(2,1)} %param.13), kind=kLoop, calls=%fused_computation.8 | loop fusion | bytes 2179072
  2.1 2.1 %copy.19 = bf16[2,576,256]{1,2,0:T(8,128)(2,1)} copy(bf16[2,576,256]{2,1,0:T(8,128)(2,1)} %param.14) | data formatting | bytes 1179648 | tf_op args[5]
  4.2 1.2 constant_dynamic-update-slice_fusion.3
  5.4 0.0 copy-done.4
  5.4 0.1 constant_dynamic-update-slice_fusion.2
  5.5 2.2 %reshape.12 = bf16[2,9,2,64,64]{3,2,1,4,0:T(2,128)(2,1)} reshape(bf16[2,1152,64]{1,2,0:T(8,128)(2,1)} %param.16) | data formatting | bytes 589824 | tf_op jit(solution)/shard_map/reshape | solution.py:378
  7.6 0.0 copy-start
  7.6 0.0 copy-start.3
  7.7 3.4 %fusion = (bf16[2,9,1,64,64]{3,2,1,4,0:T(2,128)(2,1)}, bf16[2,9,1,64,64]{3,2,1,4,0:T(2,128)(2,1)}) fusion(bf16[2,9,2,64,64]{3,2,1,4,0:T(2,128)(2,1)} %reshape.12), kind=kLoop, calls=%fused_computation.9 | loop fusion | bytes 589824 | tf_op jit(solution)/shard_map/slice | solution.py:382
  11.0 1.9 %copy.22 = bf16[2,9,1,64,64]{4,3,1,0,2:T(8,128)(2,1)} copy(bf16[2,9,1,64,64]{3,2,1,4,0:T(2,128)(2,1)} %get-tuple-element.4) | data formatting | bytes 294912
  12.9 1.8 %copy.20 = bf16[2,576,64]{1,2,0:T(8,128)(2,1)} copy(bf16[2,576,64]{2,1,0:T(8,128)(2,1)} %bitcast.12) | data formatting | bytes 294912 | tf_op jit(solution)/shard_map/reshape;squeeze | solution.py:382
  14.7 0.9 constant_dynamic-update-slice_fusion.1
  15.7 0.8 reshape.13
  16.5 0.1 fusion.1
  16.7 1.9 %copy.24 = bf16[2,9,1,64,64]{4,3,1,0,2:T(8,128)(2,1)} copy(bf16[2,9,1,64,64]{3,2,1,4,0:T(2,128)(2,1)} %get-tuple-element.3) | data formatting | bytes 294912
  18.6 1.8 %copy.21 = bf16[2,576,64]{1,2,0:T(8,128)(2,1)} copy(bf16[2,576,64]{2,1,0:T(8,128)(2,1)} %bitcast.13) | data formatting | bytes 294912 | tf_op jit(solution)/shard_map/reshape;squeeze | solution.py:382
  20.4 0.9 constant_dynamic-update-slice_fusion
  21.4 0.0 copy-done
  21.4 0.0 copy-done.3
  21.4 0.0 copy-start.1
  21.4 0.9 copy-done.1
  22.3 0.0 copy-start.2
  22.3 0.9 copy-done.2
  23.3 110.3 %shard_map.112 = (bf16[2,4,2,64,128]{4,3,2,1,0:T(8,128)(2,1)S(1)}, bf16[2,4,2,64,128]{4,3,2,1,0:T(8,128)(2,1)S(1)}, bf16[1,4,2,64,128]{4,3,2,1,0:T(8,128)(2,1)S(1)}) custom-call(bf16[3,4,2,64,128]{4,3,2,1,0:T(8,128)(2,1)S(1)} %copy-done, bf16[2,4,2,64,128]{4,3,2,1,0:T(8,128)(2,1)S(1)} %copy-done.1, bf16[2,4,2,64,128]{4,3,2,1,0:T(8,128)(2,1)S(1)} %copy-done.2, ...), custom_call_target="tpu_custom_call" | custom-call | tf_op jit(solution)/shard_map/pallas_call | solution.py:401
  133.6 0.7 copy.37
  134.3 0.7 copy.38
  135.0 0.7 copy.39
  (3 shorter events, 0.1 us)
Async XLA Ops:
  0.6 4.8 %copy-start.4 = (bf16[2,576,192]{1,2,0:T(8,128)(2,1)S(1)}, bf16[2,576,192]{1,2,0:T(8,128)(2,1)}, u32[]{:S(2)}) copy-start(bf16[2,576,192]{1,2,0:T(8,128)(2,1)} %param.15) | copy-start | bytes 1327108
  7.6 13.7 %copy-start = (bf16[3,4,2,64,128]{4,3,2,1,0:T(8,128)(2,1)S(1)}, bf16[3,4,2,64,128]{4,3,2,1,0:T(8,128)(2,1)}, u32[]{:S(2)}) copy-start(bf16[3,4,2,64,128]{4,3,2,1,0:T(8,128)(2,1)} %frames.1) | copy-start | bytes 1179652
  7.6 13.7 %copy-start.3 = (bf16[4,2,64,128]{3,2,1,0:T(8,128)(2,1)S(1)}, bf16[4,2,64,128]{3,2,1,0:T(8,128)(2,1)}, u32[]{:S(2)}) copy-start(bf16[4,2,64,128]{3,2,1,0:T(8,128)(2,1)} %memory.1) | copy-start | bytes 393220
  21.4 1.0 copy-start.1
  22.3 0.9 copy-start.2

commit v2 on v1

--- a/solution.py
+++ b/solution.py
@@ -18,9 +18,9 @@
 
 def kernel(
     rows_total, layers, steps,
-    frames, hidden, cell, memory, weights,
+    frames, hidden, cell, memory, w_x, w_h, w_m, w_o, w_l,
     hid_out, cell_out, mem_out,
-    taps, wbuf, land_h, land_c, land_cs, land_m, land_f,
+    taps, pair, b_x, b_h, b_m, b_o, b_l, land_h, land_c, land_cs, land_m, land_f,
     h_send, h_land, m_send, m_land, cell_state, mem_state, cell_last, acc_h, acc_m, acc_o,
     r_w, s_w, r_h, s_h, s_hc, r_c, r_cs, s_c, s_cc, r_m, s_m, r_f, s_f,
     r_hl, s_hl, r_ml, s_ml, r_out, s_out, l_out,
@@ -33,7 +33,8 @@
     cells = layers * steps
     tap = 3 * ch
     span = band + 4
-    t_frame, t_mem, t_cell = 0, layers + 1, layers + 2
+    t_frame, t_mem = 0, layers + 1
+    weights = ((w_x, b_x), (w_h, b_h), (w_m, b_m), (w_o, b_o), (w_l, b_l))
     has_up, has_down = row > 0, row < rows_total - 1
     up, down = lax.rem(row + rows_total - 1, rows_total), lax.rem(row + 1, rows_total)
 
@@ -51,10 +52,19 @@
 
     lane = lax.broadcasted_iota(jnp.int32, (ch, width), 1)
 
-    def put_taps(index, r, s, value):
+    def shifts(value):
         wide = value.astype(F32)
         left = jnp.where(lane == 0, 0.0, pltpu.roll(wide, 1, 1)).astype(BF16)
         right = jnp.where(lane == width - 1, 0.0, pltpu.roll(wide, width - 1, 1)).astype(BF16)
+        return left, value, right
+
+    def put_pair(half, r, s, three):
+        for b in range(3):
+            start = (r - 1) * 2 * tap + (2 * b + half) * ch
+            pair[start : start + ch, s * width : (s + 1) * width] = three[b]
+
+    def put_taps(index, r, s, value, three=None):
+        left, _, right = three or shifts(value)
         cols = slice(s * width, (s + 1) * width)
         taps[index, r * tap : r * tap + ch, cols] = left
         taps[index, r * tap + ch : r * tap + 2 * ch, cols] = value.astype(BF16)
@@ -77,7 +87,7 @@
             pl.semaphore_signal(barrier, inc=1, device_id=to(c, down), device_id_type=MESH)
 
     edge = 2 * tap
-    for index in range(layers + 3):
+    for index in range(layers + 2):
         taps[index, :edge, :] = jnp.zeros((edge, taps.shape[2]), BF16)
         taps[index, (span - 2) * tap :, :] = jnp.zeros((edge, taps.shape[2]), BF16)
     mem_state[0] = jnp.zeros(mem_state.shape[1:], BF16)
@@ -95,15 +105,16 @@
     def center_copies(j):
         layer = core * local_layers + j
         local = [
-            pltpu.make_async_copy(weights.at[j], wbuf.at[layer], r_w.at[layer]),
             pltpu.make_async_copy(hidden.at[j, mine], land_h.at[layer, 1], r_h.at[layer, 1]),
             pltpu.make_async_copy(cell.at[j, mine], land_c.at[layer], r_c.at[layer]),
         ]
         far = [
-            remote(weights.at[j], wbuf.at[layer], s_w.at[j], r_w.at[layer], other, row),
             remote(hidden.at[j, theirs], land_h.at[layer, 1], s_hc.at[j], r_h.at[layer, 1], other, row),
             remote(cell.at[j, theirs], land_c.at[layer], s_cc.at[j], r_c.at[layer], other, row),
         ]
+        for n, (w, b) in enumerate(weights):
+            local.append(pltpu.make_async_copy(w.at[j], b.at[layer], r_w.at[layer, n]))
+            far.append(remote(w.at[j], b.at[layer], s_w.at[j, n], r_w.at[layer, n], other, row))
         return local, far
 
     def halo_copies(j, side):
@@ -189,7 +200,8 @@
 
         @pl.when(k < layers)
         def _():
-            arrived(wbuf.at[layer], r_w.at[layer])
+            for n, (_, b) in enumerate(weights):
+                arrived(b.at[layer], r_w.at[layer, n])
             arrived(land_h.at[layer, 1], r_h.at[layer, 1])
             arrived(land_c.at[layer], r_c.at[layer])
             for s in range(seqs):
@@ -225,9 +237,9 @@
                         for r in range(2):
                             put_taps(t_frame, first + r, s, land_f[t, side, s, r])
 
-        w_h = wbuf[layer, 7 * ch : 11 * ch, :]
+        h_w = b_h[layer]
         for r in range(1, band + 3):
-            acc_h[r - 1] = jnp.dot(w_h, window(layer + 1, r), preferred_element_type=F32)
+            acc_h[r - 1] = jnp.dot(h_w, window(layer + 1, r), preferred_element_type=F32)
 
         for side, there in from_sides:
 
@@ -239,9 +251,9 @@
                     for s in range(seqs):
                         put_taps(t_mem, 0 if side == 0 else span - 1, s, m_land[prev, side, s])
 
-        w_m = wbuf[layer, 11 * ch : 14 * ch, :]
+        m_w = b_m[layer]
         for r in range(1, band + 3):
-            acc_m[r - 1] = jnp.dot(w_m, window(t_mem, r), preferred_element_type=F32)
+            acc_m[r - 1] = jnp.dot(m_w, window(t_mem, r), preferred_element_type=F32)
 
         for side, there in from_sides:
 
@@ -255,9 +267,9 @@
                         for r in range(2):
                             put_taps(before + 1, first + r, s, h_land[prev, side, s, r])
 
-        w_x = wbuf[layer, : 7 * ch, :]
+        x_w = b_x[layer]
         for r in range(1, band + 3):
-            a = jnp.dot(w_x, window(layer, r), preferred_element_type=F32)
+            a = jnp.dot(x_w, window(layer, r), preferred_element_type=F32)
             q = r - 1
             part = lambda n: a[n * ch : (n + 1) * ch]
             of_h = lambda n: acc_h[q, n * ch : (n + 1) * ch, :]
@@ -281,8 +293,10 @@
             own = 2 <= r < band + 2
             for s in range(seqs):
                 cols = slice(s * width, (s + 1) * width)
-                put_taps(t_cell, r, s, c_new[:, cols])
-                put_taps(t_mem, r, s, m_new[:, cols])
+                three = shifts(m_new[:, cols])
+                put_pair(0, r, s, shifts(c_new[:, cols]))
+                put_pair(1, r, s, three)
+                put_taps(t_mem, r, s, m_new[:, cols], three)
                 if own:
                     cell_last[layer, s, r - 2] = c_new[:, cols]
                     m_send[k, s, r - 2] = m_new[:, cols]
@@ -297,12 +311,14 @@
                 def _():
                     m_copy(k, side).start()
 
-        w_c = wbuf[layer, 14 * ch : 16 * ch, :]
-        w_n = wbuf[layer, 16 * ch : 18 * ch, :]
+        o_w = b_o[layer]
+        l_w = b_l[layer]
         for r in range(2, band + 2):
-            both = jnp.dot(w_c, window(t_cell, r), preferred_element_type=F32)
-            both = both + jnp.dot(w_n, window(t_mem, r), preferred_element_type=F32)
-            h_new = (sig(acc_o[r - 2] + both[:ch]) * jnp.tanh(both[ch:])).astype(BF16)
+            start = (r - 2) * 2 * tap
+            middle = start + 2 * tap + 2 * ch
+            gate = jnp.dot(o_w, pair[start : start + 6 * tap, :], preferred_element_type=F32)
+            mixed = jnp.dot(l_w, pair[middle : middle + 2 * ch, :], preferred_element_type=F32)
+            h_new = (sig(acc_o[r - 2] + gate) * jnp.tanh(mixed)).astype(BF16)
             for s in range(seqs):
                 h_send[k, s, r - 2] = h_new[:, s * width : (s + 1) * width]
 
@@ -371,20 +387,6 @@
     arrived(mem_out.at[0, theirs], r_out.at[2])
 
 
-def pack(w_x, w_h, w_m, w_o, w_last):
-    layers, depth, _ = w_x.shape
-    ch = w_last.shape[2]
-    taps = depth // ch
-    split = w_o.reshape(layers, taps, 2, ch, ch)
-    mix = w_last.reshape(layers, 2, ch, ch)
-    pieces = [w_x, w_h, w_m]
-    for half in range(2):
-        pieces.append(split[:, :, half].reshape(layers, depth, ch))
-        middle = (taps // 2) * ch
-        pieces.append(jnp.pad(mix[:, half], ((0, 0), (middle, depth - middle - ch), (0, 0))))
-    return jnp.concatenate(pieces, axis=2).transpose(0, 2, 1)
-
-
 def on_device(rows_total, cores, frames, hidden_in, cell_in, memory_in, w_x, w_h, w_m, w_o, w_last):
     steps = frames.shape[0]
     local_layers, seqs_all, band, ch, width = hidden_in.shape
@@ -392,7 +394,7 @@
     seqs = seqs_all // cores
     cells = layers * steps
     lanes = seqs * width
-    weights = pack(w_x, w_h, w_m, w_o, w_last)
+    weights = [w.transpose(0, 2, 1) for w in (w_x, w_h, w_m, w_o, w_last)]
     block = (seqs, band, ch, width)
     dma = pltpu.SemaphoreType.DMA
     vm = lambda *shape: pltpu.VMEM(shape, BF16)
@@ -405,11 +407,12 @@
             jax.ShapeDtypeStruct(cell_in.shape, BF16),
             jax.ShapeDtypeStruct((1,) + memory_in.shape, BF16),
         ),
-        in_specs=[in_vmem] * 4 + [pl.BlockSpec(memory_space=pl.ANY)],
+        in_specs=[in_vmem] * 4 + [pl.BlockSpec(memory_space=pl.ANY)] * len(weights),
         out_specs=(in_vmem,) * 3,
         scratch_shapes=[
-            vm(layers + 3, (band + 4) * 3 * ch, lanes),
-            vm(layers, *weights.shape[1:]),
+            vm(layers + 2, (band + 4) * 3 * ch, lanes),
+            vm((band + 2) * 6 * ch, lanes),
+            *[vm(layers, *w.shape[1:]) for w in weights],
             vm(layers, 3, *block),
             vm(layers, *block),
             vm(layers, 2, seqs, ch, width),
@@ -425,7 +428,7 @@
             vf(band + 2, 4 * ch, lanes),
             vf(band + 2, 3 * ch, lanes),
             vf(band, ch, lanes),
-            dma((layers,)), dma((local_layers,)),
+            dma((layers, len(weights))), dma((local_layers, len(weights))),
             dma((layers, 3)), dma((local_layers, cores, 2)), dma((local_layers,)),
             dma((layers,)), dma((layers, 2)), dma((local_layers, cores, 2)), dma((local_layers,)),
             dma((2,)), dma((2,)),
@@ -437,7 +440,7 @@
         compiler_params=pltpu.CompilerParams(
             collective_id=0, has_side_effects=True, vmem_limit_bytes=48 * 1024 * 1024
         ),
-    )(frames, hidden_in, cell_in, memory_in, weights)
+    )(frames, hidden_in, cell_in, memory_in, *weights)
 
 
 def solution(mesh):

time: 137 us -> 122 us (0.89)
  local copies, waits for them, and re-layouts: 24.6 us -> 9.31 us
    unnamed x22 -> x20, local copies, waits for them, and re-layouts: 14.5 us -> 9.31 us
    another operation x2 -> x0, local copies, waits for them, and re-layouts: 3.56 us -> none  [pack(): pieces.append(split[:, :, half].reshape(layers, depth, ch))]
    slice x2 -> x0, local copies, waits for them, and re-layouts: 3.47 us -> none  [the longest x1 3.37 us: pack(): pieces.append(split[:, :, half].reshape(layers, depth, ch))]
    reshape x2 -> x0, local copies, waits for them, and re-layouts: 3.02 us -> none  [the longest x1 2.18 us: pack(): split = w_o.reshape(layers, taps, 2, ch, ch)]
where the time goes in v2:
time: 122 us; the launch traced here: 120 us
  Pallas kernels  110 us (90%)
  local copies, waits for them, and re-layouts  9.31 us (8%)
    pallas_call x1, Pallas kernels, on_device(): pl.pallas_call(functools.partial(kernel, rows_total, layers, steps), out_...  110 us
    unnamed x20, local copies, waits for them, and re-layouts  9.31 us

profile of v2, /device:TPU:0, one launch (start us, length us, event | category | flops | bytes accessed | tf_op | source)
XLA Modules:
  0.0 119.7 jit_solution(18298002064076087432)
XLA Ops:
  0.6 0.0 copy-start.7
  0.6 0.0 copy-start
  0.7 1.5 %copy.12 = bf16[2,576,256]{1,2,0:T(8,128)(2,1)S(1)} copy(bf16[2,576,256]{2,1,0:T(8,128)(2,1)} %param.14) | data formatting | bytes 1179648 | tf_op args[5]
  2.1 0.0 copy-done.7
  2.1 0.0 copy-done
  2.1 0.0 copy-start.1
  2.1 1.0 copy-done.1
  3.2 0.0 copy-start.2
  3.2 1.0 copy-done.2
  4.2 0.0 copy-start.3
  4.2 1.0 copy-done.3
  5.1 0.0 copy-start.4
  5.1 0.9 copy-done.4
  6.1 0.0 copy-start.5
  6.1 0.9 copy-done.5
  7.0 0.0 copy-start.6
  7.0 0.9 copy-done.6
  7.9 109.7 %shard_map.112 = (bf16[2,4,2,64,128]{4,3,2,1,0:T(8,128)(2,1)S(1)}, bf16[2,4,2,64,128]{4,3,2,1,0:T(8,128)(2,1)S(1)}, bf16[1,4,2,64,128]{4,3,2,1,0:T(8,128)(2,1)S(1)}) custom-call(bf16[3,4,2,64,128]{4,3,2,1,0:T(8,128)(2,1)S(1)} %copy-done.2, bf16[2,4,2,64,128]{4,3,2,1,0:T(8,128)(2,1)S(1)} %copy-done.4, bf16[2,4,2,64,128]{4,3,2,1,0:T(8,128)(2,1)S(1)} %copy-done.5, ...), custom_call_target="tpu_custom_call" | custom-call | tf_op jit(solution)/shard_map/pallas_call | solution.py:403
  117.6 0.7 copy.16
  118.3 0.7 copy.17
  119.0 0.7 copy.18
Async XLA Ops:
  0.6 1.5 %copy-start.7 = (bf16[2,128,64]{1,2,0:T(8,128)(2,1)S(1)}, bf16[2,128,64]{1,2,0:T(8,128)(2,1)}, u32[]{:S(2)}) copy-start(bf16[2,128,64]{1,2,0:T(8,128)(2,1)} %param.17) | copy-start | bytes 98308
  0.6 1.5 %copy-start = (bf16[2,576,448]{1,2,0:T(8,128)(2,1)S(1)}, bf16[2,576,448]{1,2,0:T(8,128)(2,1)}, u32[]{:S(2)}) copy-start(bf16[2,576,448]{1,2,0:T(8,128)(2,1)} %param.13) | copy-start | bytes 3096580
  2.1 1.0 copy-start.1
  3.2 1.0 copy-start.2
  4.2 1.0 copy-start.3
  5.1 0.9 copy-start.4
  6.1 0.9 copy-start.5
  7.0 0.9 copy-start.6

commit v3 on v2

--- a/solution.py
+++ b/solution.py
@@ -20,9 +20,9 @@
     rows_total, layers, steps,
     frames, hidden, cell, memory, w_x, w_h, w_m, w_o, w_l,
     hid_out, cell_out, mem_out,
-    taps, pair, b_x, b_h, b_m, b_o, b_l, land_h, land_c, land_cs, land_m, land_f,
+    taps, pair, b_x, b_h, b_m, b_o, b_l, land_h, land_c, land_cs, land_m, land_f, m_in, f_in,
     h_send, h_land, m_send, m_land, cell_state, mem_state, cell_last, acc_h, acc_m, acc_o,
-    r_w, s_w, r_h, s_h, s_hc, r_c, r_cs, s_c, s_cc, r_m, s_m, r_f, s_f,
+    r_w, s_w, r_h, s_h, s_hc, r_c, r_cs, s_c, s_cc, r_m, s_m, r_f, s_f, l_m, l_f,
     r_hl, s_hl, r_ml, s_ml, r_out, s_out, l_out,
 ):
     core, row = lax.axis_index("layer"), lax.axis_index("rows")
@@ -141,6 +141,12 @@
     sides = ((0, has_down), (1, has_up))
     from_sides = ((0, has_up), (1, has_down))
 
+    own_memory = pltpu.make_async_copy(memory.at[mine], m_in, l_m.at[0])
+    own_memory.start()
+    own_frames = [pltpu.make_async_copy(frames.at[t, mine], f_in.at[t], l_f.at[t]) for t in range(steps)]
+    for copy in own_frames:
+        copy.start()
+
     for j in range(local_layers):
         local, far = center_copies(j)
         for copy in far + local:
@@ -162,10 +168,12 @@
             def _():
                 frame_copy(t, side).start()
 
+    for copy in [own_memory] + own_frames:
+        copy.wait()
     for s in range(seqs):
         cols = slice(s * width, (s + 1) * width)
         for r in range(band):
-            value = memory[core * seqs + s, r]
+            value = m_in[s, r]
             put_taps(t_mem, 2 + r, s, value)
             mem_state[1 + r, :, cols] = value
     for side, there in from_sides:
@@ -226,7 +234,7 @@
         def _():
             for s in range(seqs):
                 for r in range(band):
-                    put_taps(t_frame, 2 + r, s, frames[t, core * seqs + s, r])
+                    put_taps(t_frame, 2 + r, s, f_in[t, s, r])
             for side, there in from_sides:
 
                 @pl.when(there)
@@ -255,8 +263,7 @@
         for r in range(1, band + 3):
             acc_m[r - 1] = jnp.dot(m_w, window(t_mem, r), preferred_element_type=F32)
 
-        for side, there in from_sides:
-
+        def take_rows(side, there):
             @pl.when(there)
             def _():
                 @pl.when(k > 0)
@@ -269,6 +276,10 @@
 
         x_w = b_x[layer]
         for r in range(1, band + 3):
+            if r == 1:
+                take_rows(0, has_up)
+            if r == band + 1:
+                take_rows(1, has_down)
             a = jnp.dot(x_w, window(layer, r), preferred_element_type=F32)
             q = r - 1
             part = lambda n: a[n * ch : (n + 1) * ch]
@@ -407,7 +418,7 @@
             jax.ShapeDtypeStruct(cell_in.shape, BF16),
             jax.ShapeDtypeStruct((1,) + memory_in.shape, BF16),
         ),
-        in_specs=[in_vmem] * 4 + [pl.BlockSpec(memory_space=pl.ANY)] * len(weights),
+        in_specs=[pl.BlockSpec(memory_space=pl.ANY)] * (4 + len(weights)),
         out_specs=(in_vmem,) * 3,
         scratch_shapes=[
             vm(layers + 2, (band + 4) * 3 * ch, lanes),
@@ -418,6 +429,8 @@
             vm(layers, 2, seqs, ch, width),
             vm(2, *block),
             vm(steps, 2, *block),
+            vm(*block),
+            vm(steps, *block),
             vm(cells, *block),
             vm(cells, 2, *block),
             vm(cells, *block),
@@ -432,13 +445,13 @@
             dma((layers, 3)), dma((local_layers, cores, 2)), dma((local_layers,)),
             dma((layers,)), dma((layers, 2)), dma((local_layers, cores, 2)), dma((local_layers,)),
             dma((2,)), dma((2,)),
-            dma((steps, 2)), dma((steps, 2)),
+            dma((steps, 2)), dma((steps, 2)), dma((1,)), dma((steps,)),
             dma((cells, 2)), dma((cells, 2)),
             dma((cells, 2)), dma((cells, 2)),
             dma((3,)), dma((3,)), dma((3,)),
         ],
         compiler_params=pltpu.CompilerParams(
-            collective_id=0, has_side_effects=True, vmem_limit_bytes=48 * 1024 * 1024
+            collective_id=0, has_side_effects=True, vmem_limit_bytes=62 * 1024 * 1024
         ),
     )(frames, hidden_in, cell_in, memory_in, *weights)
 

time: 122 us -> 123 us (level); the launches traced: 120 us -> 123 us
  Pallas kernels: 110 us -> 115 us
  local copies, waits for them, and re-layouts: 9.31 us -> 7.06 us
    pallas_call x1, Pallas kernels: 110 us -> 115 us  [on_device(): pl.pallas_call(functools.partial(kernel, rows_total, layers, steps), out_...]
    unnamed x20 -> x4, local copies, waits for them, and re-layouts: 9.31 us -> 7.06 us
where the time goes in v3:
time: 123 us
  Pallas kernels  115 us (93%)
  local copies, waits for them, and re-layouts  7.06 us (6%)
    pallas_call x1, Pallas kernels, on_device(): pl.pallas_call(functools.partial(kernel, rows_total, layers, steps), out_...  115 us
    unnamed x4, local copies, waits for them, and re-layouts  7.06 us

profile of v3, /device:TPU:0, one launch (start us, length us, event | category | flops | bytes accessed | tf_op | source)
XLA Modules:
  0.0 122.5 jit_solution(13079437720066358494)
XLA Ops:
  0.6 2.2 %copy.12 = bf16[2,576,256]{1,2,0:T(8,128)(2,1)} copy(bf16[2,576,256]{2,1,0:T(8,128)(2,1)} %param.14) | data formatting | bytes 1179648 | tf_op args[5]
  2.8 114.8 %shard_map.112 = (bf16[2,4,2,64,128]{4,3,2,1,0:T(8,128)(2,1)}, bf16[2,4,2,64,128]{4,3,2,1,0:T(8,128)(2,1)}, bf16[1,4,2,64,128]{4,3,2,1,0:T(8,128)(2,1)}) custom-call(bf16[3,4,2,64,128]{4,3,2,1,0:T(8,128)(2,1)} %frames.1, bf16[2,4,2,64,128]{4,3,2,1,0:T(8,128)(2,1)} %hidden.1, bf16[2,4,2,64,128]{4,3,2,1,0:T(8,128)(2,1)} %cell.1, ...), custom_call_target="tpu_custom_call" | custom-call | tf_op jit(solution)/shard_map/pallas_call | solution.py:414
  117.6 1.7 %copy.16 = bf16[2,4,2,64,128]{4,3,2,1,0:T(8,128)(2,1)} copy(bf16[2,4,2,64,128]{4,3,2,1,0:T(8,128)(2,1)} %get-tuple-element.6) | data formatting | bytes 524288
  119.3 1.7 %copy.17 = bf16[2,4,2,64,128]{4,3,2,1,0:T(8,128)(2,1)} copy(bf16[2,4,2,64,128]{4,3,2,1,0:T(8,128)(2,1)} %get-tuple-element.7) | data formatting | bytes 524288
  121.0 1.6 %copy.18 = bf16[1,4,2,64,128]{4,3,2,1,0:T(8,128)(2,1)} copy(bf16[1,4,2,64,128]{4,3,2,1,0:T(8,128)(2,1)} %get-tuple-element.8) | data formatting | bytes 262144
